TPU v7x, 256 devices: a whole 4x4x8 slice. The times are simulated.
256 devices in a mesh: seq: 32 (over z_lo, x, y), head: 8 (over z_hi, core).
Axes of the slice: x: 4, y: 4, z: 8 (z_hi: 4, z_lo: 2; z = z_hi * 2 + z_lo), core: 2. Of those that a mesh axis runs over, the one named last changes fastest.
Arguments:
- x_in: bfloat16 [16384, 4096], P('seq', 'head'), may hold values from -6 to 6
- b_proj: bfloat16 [16384, 1024], P('seq', 'head'), may hold values from -0.125 to 0.125
- c_proj: bfloat16 [16384, 1024], P('seq', 'head'), may hold values from -0.125 to 0.125
- decay: float32 [64, 16384], P('head', 'seq'), may hold values from 0.55 to 1, as said below
- d_skip: float32 [64], P('head'), may hold values from 0.5 to 1.5
- block_states: float32 [64, 64, 64, 128], P('seq', 'head'), may hold values from -6 to 6
- grad_out: bfloat16 [16384, 4096], P('seq', 'head'), may hold values from -6 to 6
- w_x: bfloat16 [4096, 4096], P(None, 'head'), may hold values from -0.09375 to 0.09375
- w_b: bfloat16 [4096, 1024], P(None, 'head'), may hold values from -0.09375 to 0.09375
- w_c: bfloat16 [4096, 1024], P(None, 'head'), may hold values from -0.09375 to 0.09375
Outputs:
- grad_input: bfloat16 [4096, 16384], P('head', 'seq')
- grad_decay: float32 [64, 16384], P('head', 'seq')
Inputs may be any that keep to these rules, and one draw needn't show every extreme that they name: `decay`: on some heads the product of the decays over the whole sequence stays above a tenth; every other head loses half a percent or more at each step.
All inputs are finite; a program needn't handle non-finite values.
Results may differ from a plain program's by a relative error of at most 0.017.
Values may be sent and summed in bfloat16 or wider, within the bound.
A program may use at most 128 MiB of HBM per device.

v0:
```python
import math

import jax
import jax.numpy as jnp
from jax import lax
from jax.sharding import PartitionSpec as P

P_SIZE = 64
N = 128
Q = 256


highest = lax.Precision.HIGHEST
contract_last = (((1,), (1,)), ((), ()))


def carried_in(array, axis, combine, identity):
    size, mine = (lax.axis_size(axis), lax.axis_index(axis))
    everything = jax.tree.map(lambda part: lax.all_gather(part, axis), array)
    start = jax.tree.map(
        lambda part, zero: jnp.broadcast_to(jnp.asarray(zero, part.dtype), part.shape),
        array,
        identity,
    )

    def turn(k, before):
        at = size - 1 - k
        reached = at > mine
        new = combine(before, jax.tree.map(lambda part: part[at], everything))
        return jax.tree.map(lambda a, b: jnp.where(reached, a, b), new, before)

    return lax.fori_loop(0, size, turn, start)


def expand_groups(source, per_group):
    length, group_count, columns = source.shape
    return jnp.broadcast_to(
        source[:, :, None, :], (length, group_count, per_group, columns)
    ).reshape(length, group_count * per_group, columns)


def suffix_sum(values):
    positions = jnp.arange(values.shape[-1])
    suffix_mask = (positions[:, None] >= positions[None, :]).astype(jnp.float32)
    return jnp.dot(values, suffix_mask, precision=highest)


def block_parts(inputs, upstream, b_rows, c_rows, log_decay, saved, x_low, up_low, b_low, c_low):
    head_count = inputs.shape[1]
    group_count = b_rows.shape[1]
    per_group = head_count // group_count
    block_len = inputs.shape[0]
    positions = jnp.arange(block_len)
    causal = positions[:, None] >= positions[None, :]
    cum_log = jnp.cumsum(log_decay, axis=1)
    log_gaps = cum_log[:, :, None] - cum_log[:, None, :]
    decay_mat = jnp.where(causal, jnp.exp(jnp.where(causal, log_gaps, 0.0)), 0.0)
    intersection = jnp.einsum("ign,jgn->gij", c_low, b_low, preferred_element_type=jnp.float32)
    head_intersection = jnp.broadcast_to(
        intersection[:, None], (group_count, per_group, block_len, block_len)
    ).reshape(head_count, block_len, block_len)
    b_heads = expand_groups(b_rows, per_group)
    c_heads = expand_groups(c_rows, per_group)
    forward_mat = decay_mat * head_intersection
    decayed_product = decay_mat * jnp.einsum(
        "ihp,jhp->hij", up_low, x_low, preferred_element_type=jnp.float32
    )
    from_start = jnp.exp(cum_log).T[:, :, None]
    to_end = jnp.exp(cum_log[:, -1:] - cum_log).T[:, :, None]
    grad_x0 = jnp.einsum("hij,ihp->jhp", forward_mat, upstream, precision=highest)
    grad_b0 = jnp.einsum("hij,ihn->jhn", decayed_product, c_heads, precision=highest)
    grad_c0 = jnp.einsum(
        "hij,jhn->ihn", decayed_product, b_heads, precision=highest
    ) + from_start * jnp.einsum("ihp,hpn->ihn", upstream, saved, precision=highest)
    output = jnp.einsum(
        "hij,jhp->ihp", forward_mat, inputs, precision=highest
    ) + from_start * jnp.einsum("ihn,hpn->ihp", c_heads, saved, precision=highest)
    terms_base = (jnp.sum(upstream * output, axis=2) - jnp.sum(inputs * grad_x0, axis=2)).T
    adj_local = jnp.einsum("ihp,ihn->hpn", upstream * from_start, c_heads, precision=highest)
    coupling = jnp.einsum("ihp,ihn->hpn", inputs * to_end, b_heads, precision=highest)
    through = jnp.exp(cum_log[:, -1])
    return (grad_x0, grad_b0, grad_c0, terms_base, through, adj_local, coupling, to_end)


def right_terms(inputs, b_rows, to_end, adjoint):
    per_group = inputs.shape[1] // b_rows.shape[1]
    b_heads = expand_groups(b_rows, per_group)
    grad_xr = to_end * jnp.einsum("jhn,hpn->jhp", b_heads, adjoint, precision=highest)
    grad_br = to_end * jnp.einsum("jhp,hpn->jhn", inputs, adjoint, precision=highest)
    terms_right = -jnp.sum(inputs * grad_xr, axis=2).T
    return (grad_xr, grad_br, terms_right)


def combine_state(earlier, latter):
    return (latter[0] * earlier[0], latter[1] + latter[0][..., None, None] * earlier[1])


def add_sums(earlier, latter):
    return earlier + latter


def body(x_in, b_proj, c_proj, decay, d_skip, block_states, grad_out, w_x, w_b, w_c):
    tok_count = x_in.shape[0]
    head_count = decay.shape[0]
    group_count = b_proj.shape[1] // N
    blocks = tok_count // Q
    x_low = x_in.reshape(blocks, Q, head_count, P_SIZE)
    up_low = grad_out.reshape(blocks, Q, head_count, P_SIZE)
    b_low = b_proj.reshape(blocks, Q, group_count, N)
    c_low = c_proj.reshape(blocks, Q, group_count, N)
    inputs_all = x_low.astype(jnp.float32)
    upstream_all = up_low.astype(jnp.float32)
    b_all = b_low.astype(jnp.float32)
    c_all = c_low.astype(jnp.float32)
    log_all = jnp.log(decay).reshape(head_count, blocks, Q).transpose(1, 0, 2)
    grad_x0, grad_b0, grad_c0, terms_base, through, adj_local, coupling, to_end = jax.vmap(
        block_parts
    )(inputs_all, upstream_all, b_all, c_all, log_all, block_states, x_low, up_low, b_low, c_low)
    ones_heads = jnp.ones((head_count,), jnp.float32)
    zero_heads = jnp.zeros((head_count,), jnp.float32)
    zero_states = jnp.zeros((head_count, P_SIZE, N), jnp.float32)
    adjoints = [None] * blocks
    later_totals = [None] * blocks
    summary = (through[blocks - 1], adj_local[blocks - 1])
    index_b = 0
    summary = combine_state(summary, (through[index_b], adj_local[index_b]))
    beyond = carried_in((summary[0], summary[1]), "seq", combine_state, (ones_heads, zero_states))
    cursor = beyond
    for index_b in range(blocks - 1, -1, -1):
        adjoints[index_b] = cursor[1]
        cursor = combine_state(cursor, (through[index_b], adj_local[index_b]))
    grad_xr, grad_br, terms_right = jax.vmap(right_terms)(
        inputs_all, b_all, to_end, jnp.stack(adjoints)
    )
    all_terms = terms_base + terms_right
    block_sums = jnp.sum(all_terms, axis=2)
    device_sum = jnp.sum(block_sums, axis=0)
    running = carried_in(device_sum, "seq", add_sums, zero_heads)
    for index_b in range(blocks - 1, -1, -1):
        later_totals[index_b] = running
        running = running + block_sums[index_b]
    decay_grad = suffix_sum(all_terms) + jnp.stack(later_totals)[:, :, None]
    norm_factor = 1.0 / math.sqrt(tok_count * lax.axis_size("seq"))
    grad_decay = decay_grad.transpose(1, 0, 2).reshape(head_count, tok_count) * norm_factor
    per_group = head_count // group_count
    grad_x = (
        (grad_x0 + grad_xr + d_skip[:, None] * upstream_all)
        .reshape(tok_count, head_count * P_SIZE)
        .astype(jnp.bfloat16)
    )
    grad_b = (
        (grad_b0 + grad_br)
        .reshape(tok_count, group_count, per_group, N)
        .sum(axis=2)
        .reshape(tok_count, group_count * N)
        .astype(jnp.bfloat16)
    )
    grad_c = (
        grad_c0.reshape(tok_count, group_count, per_group, N)
        .sum(axis=2)
        .reshape(tok_count, group_count * N)
        .astype(jnp.bfloat16)
    )
    partial_value = lax.dot_general(w_x, grad_x, contract_last, preferred_element_type=jnp.float32)
    partial_value = partial_value + lax.dot_general(
        w_b, grad_b, contract_last, preferred_element_type=jnp.float32
    )
    summed = lax.psum_scatter(
        (
            partial_value
            + lax.dot_general(w_c, grad_c, contract_last, preferred_element_type=jnp.float32)
        ).astype(jnp.bfloat16),
        "head",
        scatter_dimension=0,
        tiled=True,
    )
    return (summed, grad_decay)


def solution(mesh):
    return jax.shard_map(
        body,
        mesh=mesh,
        in_specs=(
            P("seq", "head"),
            P("seq", "head"),
            P("seq", "head"),
            P("head", "seq"),
            P("head"),
            P("seq", "head", None, None),
            P("seq", "head"),
            P(None, "head"),
            P(None, "head"),
            P(None, "head"),
        ),
        out_specs=(P("head", "seq"), P("head", "seq")),
        check_vma=False,
    )
```

profile of v0, /device:TPU:64, one launch (start us, length us, event | category | flops | bytes accessed | tf_op | source)
XLA Modules:
  0.0 377.0 jit_solution(13685651842326162342)
XLA Ops:
  8.1 1.1 reduce-window.6
  11.2 1.7 reshape.137
  13.5 1.1 fusion.48
  17.1 1.6 reshape.138
  19.4 1.3 dynamic-slice
  21.3 84.4 %all-gather.1 = f32[32,1,8]{2,1,0:T(1,128)} all-gather(f32[1,1,8]{2,1,0:T(1,128)} %get-tuple-element.313), channel_id=1, replica_groups=mesh['seq'=32,'head'=8] {'seq'}, dimensions={0}, use_global_device_ids=true | all-gather | bytes 1056 | tf_op jit(solution)/shard_map/all_gather | solution.py:19
  105.8 1.4 exponential_bitcast_fusion.1
  108.0 4.8 %fusion.8 = f32[2,8,256,128]{3,2,1,0:T(8,128)S(1)} fusion(f32[2,8,256,256]{3,2,1,0:T(8,128)S(1)} %fusion.69, f32[2,8,256]{2,1,0:T(8,128)S(1)} %copy-done.16, pred[256,256]{1,0:T(8,128)(4,1)S(1)} %iota_compare_fusion, f32[2,256,128]{2,1,0:T(8,128)S(1)} %copy-done.9), kind=kOutput, calls=%fused_computation.12 | convolution fusion | flops 1614807040 | bytes 6635520 | tf_op jit(solution)/shard_map/vmap(hij,jhn->ihn)/dot_general | solution.py:72
  112.8 1.9 fusion.13
  114.7 1.1 fusion.67
  115.7 9.2 %fusion.10 = f32[2,8,256,128]{3,2,1,0:T(8,128)} fusion(f32[2,8,256,256]{3,2,1,0:T(8,128)S(1)} %fusion.69, f32[2,8,256]{2,1,0:T(8,128)S(1)} %copy-done.16, pred[256,256]{1,0:T(8,128)(4,1)S(1)} %iota_compare_fusion, f32[2,256,128]{2,1,0:T(8,128)S(1)} %copy-done.5), kind=kOutput, calls=%fused_computation.13 | convolution fusion | flops 1614807040 | bytes 6635520 | tf_op jit(solution)/shard_map/vmap(hij,ihn->jhn)/dot_general | solution.py:71
  124.9 63.1 %all-gather.4.cloned.1.call-done = f32[32,8,64,128]{3,2,1,0:T(8,128)} async-done(((f32[1,8,64,128]{3,2,1,0:T(8,128)}), f32[32,8,64,128]{3,2,1,0:T(8,128)}) %all-gather.4.cloned.1.call-update) | async-done | bytes 8388624 | tf_op jit(solution)/shard_map/all_gather | solution.py:19
  188.1 56.5 %while.32 = (s32[]{:T(128)}, f32[8,64,128]{2,1,0:T(8,128)S(1)}, s32[]{:T(128)}, f32[32,8,64,128]{3,2,1,0:T(8,128)}, f32[32,8]{1,0:T(8,128)}, /*index=5*/s32[]{:T(128)}, s32[]{:T(128)}, s32[]{:T(128)}, s32[]{:T(128)}) while((s32[]{:T(128)}, f32[8,64,128]{2,1,0:T(8,128)S(1)}, s32[]{:T(128)}, f32[32,8,64,128]{3,2,1,0:T(8,128)}, ...), condition=%wide.region_3.4_spmd.clone, body=%wide.region_2.3_spmd.clone.sunk | while | flops 262152 | bytes 786703 | solution.py:32
  188.7 1.0 fusion.88
  192.3 1.0 fusion.88
  202.9 1.0 fusion.88
  204.6 1.0 fusion.88
  206.4 1.0 fusion.88
  208.2 1.0 fusion.88
  209.9 1.0 fusion.88
  211.7 1.0 fusion.88
  245.3 3.0 fusion.40
  248.3 4.6 %fusion.46 = (f32[2,256,8]{1,2,0:T(8,128)S(1)}, f32[2,256,8]{1,2,0:T(8,128)S(1)}, bf16[2,256,8,64]{1,3,2,0:T(8,128)(2,1)S(1)}) fusion(bf16[2,256,8,64]{1,3,2,0:T(8,128)(2,1)S(1)} %copy.58, f32[2,256,8,64]{1,3,2,0:T(8,128)S(1)} %fusion.40, bf16[2,256,8,64]{1,3,2,0:T(8,128)(2,1)S(1)} %copy.53, f32[8]{0:T(128)} %param.18, f32[2,256,256]{2,1,0:T(8,128)} %fusion.67, ...), kind=kOutput, calls=%fused_computation.54 | convolution fusion | flops 812113920 | bytes 3260448 | tf_op jit(solution)/shard_map/vmap(hij,ihp->jhp)/dot_general | solution.py:70
  253.6 1.7 fusion.15
  255.3 2.4 fusion.68
  257.7 1.3 fusion.70
  259.0 3.2 fusion.1
  263.3 3.2 fusion.37
  266.5 2.3 fusion.43
  269.2 96.4 %all-reduce = f32[256]{0:T(256)S(1)} all-reduce(f32[256]{0:T(256)S(1)} %dynamic-update-slice), channel_id=2, replica_groups=mesh['seq'=32,'head'=8] {'seq'}, use_global_device_ids=true, to_apply=%add | all-reduce | flops 256 | bytes 2048
  365.8 1.4 while.33
  368.1 2.0 copy.66
  (165 shorter events, 58.6 us)
Async XLA Ops:
  7.2 250.5 %copy-start = (bf16[4096,128]{1,0:T(8,128)(2,1)S(1)}, bf16[4096,128]{1,0:T(8,128)(2,1)}, u32[]{:S(2)}) copy-start(bf16[4096,128]{1,0:T(8,128)(2,1)} %param.22) | copy-start | bytes 3145732
  7.2 9.2 %copy-start.13 = (bf16[512,128]{1,0:T(8,128)(2,1)S(1)}, bf16[512,128]{1,0:T(8,128)(2,1)}, u32[]{:S(2)}) copy-start(bf16[512,128]{1,0:T(8,128)(2,1)} %param.15) | copy-start | bytes 393220
  7.2 180.9 %all-gather.4.cloned.1.call-start = ((), (), s32[]{:S(2)}) async-start(), calls=%async_computation.1 | async-start | bytes 8650752 | tf_op jit(solution)/shard_map/all_gather | solution.py:19
  9.5 1.7 copy-start.15
  9.6 1.5 copy-start.21
  11.1 5.2 %copy-start.4 = (f32[2,256,128]{2,1,0:T(8,128)}, f32[2,256,128]{2,1,0:T(8,128)S(1)}, u32[]{:S(2)}) copy-start(f32[2,256,128]{2,1,0:T(8,128)S(1)} %bitcast_convert_fusion) | copy-start | bytes 786436
  14.6 0.8 copy-start.2
  16.3 351.8 %reduce-scatter.2.cloned.1.call-start = ((), (), s32[]{:S(2)}) async-start(), calls=%async_computation.2 | async-start | bytes 4718592 | tf_op jit(solution)/shard_map/reduce_scatter | solution.py:168
  19.3 88.6 %copy-start.9 = (f32[2,256,128]{2,1,0:T(8,128)S(1)}, f32[2,256,128]{2,1,0:T(8,128)}, u32[]{:S(2)}) copy-start(f32[2,256,128]{2,1,0:T(8,128)} %convert_element_type.51) | copy-start | bytes 786436
  19.3 88.6 %copy-start.16 = (f32[2,8,256]{2,1,0:T(8,128)S(1)}, f32[2,8,256]{2,1,0:T(8,128)}, u32[]{:S(2)}) copy-start(f32[2,8,256]{2,1,0:T(8,128)} %copy-done.15) | copy-start | bytes 49156
  105.7 10.0 %copy-start.18 = (pred[256,256]{1,0:T(8,128)(4,1)}, pred[256,256]{1,0:T(8,128)(4,1)S(1)}, u32[]{:S(2)}) copy-start(pred[256,256]{1,0:T(8,128)(4,1)S(1)} %iota_compare_fusion) | copy-start | bytes 196612
  107.9 4.8 %copy-start.7 = (f32[2,8,64,128]{3,2,1,0:T(8,128)S(1)}, f32[2,8,64,128]{3,2,1,0:T(8,128)}, u32[]{:S(2)}) copy-start(f32[2,8,64,128]{3,2,1,0:T(8,128)} %param.19) | copy-start | bytes 1572868
  108.0 6.7 %copy-start.12 = (bf16[512,128]{1,0:T(8,128)(2,1)S(1)}, bf16[512,128]{1,0:T(8,128)(2,1)}, u32[]{:S(2)}) copy-start(bf16[512,128]{1,0:T(8,128)(2,1)} %param.16) | copy-start | bytes 393220
  108.0 7.8 %copy-start.5 = (f32[2,256,128]{2,1,0:T(8,128)S(1)}, f32[2,256,128]{2,1,0:T(8,128)}, u32[]{:S(2)}) copy-start(f32[2,256,128]{2,1,0:T(8,128)} %copy-done.4) | copy-start | bytes 786436
  124.9 119.7 %copy-start.3 = (f32[2,8,64,128]{3,2,1,0:T(8,128)S(1)}, f32[2,8,64,128]{3,2,1,0:T(8,128)}, u32[]{:S(2)}) copy-start(f32[2,8,64,128]{3,2,1,0:T(8,128)} %copy-done.2) | copy-start | bytes 1572868
  248.3 5.3 %copy-start.6 = (f32[2,8,256,128]{3,2,1,0:T(8,128)S(1)}, f32[2,8,256,128]{3,2,1,0:T(8,128)}, u32[]{:S(2)}) copy-start(f32[2,8,256,128]{3,2,1,0:T(8,128)} %fusion.10) | copy-start | bytes 6291460
  248.3 5.3 %copy-start.14 = (f32[2,256,8]{1,2,0:T(8,128)S(1)}, f32[2,256,8]{1,2,0:T(8,128)}, u32[]{:S(2)}) copy-start(f32[2,256,8]{1,2,0:T(8,128)} %exponential_bitcast_fusion.1) | copy-start | bytes 49156
  252.9 2.4 copy-start.1
  257.7 1.3 copy-start.10
  262.2 1.0 copy-start.11
  262.2 1.0 copy-start.17
  262.2 1.0 copy-start.19
  263.3 3.2 copy-start.8
  263.3 102.5 %copy-start.20 = (f32[8]{0:T(128)S(1)}, f32[8]{0:T(128)}, u32[]{:S(2)}) copy-start(f32[8]{0:T(128)} %custom-call.1) | copy-start | bytes 100
Sparse Core Ops, SparseCore 0:
  16.4 171.6 all-gather.3
  262.4 59.0 reduce-scatter.1
where the time goes:
time: 379 us; the launch traced here: 377 us
  blocking collectives  181 us (48%)
  waiting for transfers between devices  63.2 us (17%)
  matrix products  41.2 us (11%)
  other arithmetic  40.8 us (11%)
  local copies, waits for them, and re-layouts  33.9 us (9%)
  between operations  15.1 us (4%)
    unnamed x1, blocking collectives  96.4 us
    all_gather x1, blocking collectives, carried_in(): everything = jax.tree.map(lambda part: lax.all_gather(part, axis), array)  84.4 us
    all_gather x1, waiting for transfers between devices, carried_in(): everything = jax.tree.map(lambda part: lax.all_gather(part, axis), array)  63.1 us
    select_n x64, other arithmetic, turn(): return jax.tree.map(lambda a, b: jnp.where(reached, a, b), new, before)  34.1 us
    mul x32, local copies, waits for them, and re-layouts, combine_state(): latter[0][..., None, None] * earlier[1]  22 us
    dot_general x1, matrix products, block_parts(): jnp.einsum('hij,ihn->jhn', decayed_product, c_heads, precision=highest)  9.18 us
  transfers between devices with their start and end apart: 2, of which 1 were waited for; matrix products, arithmetic and copies ran while one was open for 8% of the time, Pallas kernels for 0%

commit v1 on v0

v1 whole, which is shorter than its diff:
```python
import math

import jax
import jax.numpy as jnp
from jax import lax
from jax.experimental import pallas as pl
from jax.experimental.pallas import tpu as pltpu
from jax.sharding import PartitionSpec as P

SEQ = 32
HEAD = 8
TOK = 512
Q = 256
NH = 8
PS = 64
N = 128
HP = NH * PS
KOWN = HP + 2 * N
ROWS = 512
TM = 128
SL = HP // SEQ

MESH = pl.DeviceIdType.MESH
f32 = jnp.float32
bf16 = jnp.bfloat16

TN = (((0,), (0,)), ((), ()))
NT = (((1,), (1,)), ((), ()))


def dot(a, b, dims=(((1,), (0,)), ((), ()))):
    return lax.dot_general(a, b, dims, preferred_element_type=f32)


def split3(v):
    hi = v.astype(bf16).astype(f32)
    rest = v - hi
    mid = rest.astype(bf16).astype(f32)
    low = rest - mid
    return jnp.concatenate([hi, mid, low], axis=0).astype(bf16)


def exact_dot(v, mask):
    rows = v.shape[0]
    out = dot(split3(v), mask)
    return out[0:rows] + out[rows : 2 * rows] + out[2 * rows : 3 * rows]


def kernel(
    x_hbm, b_hbm, c_hbm, dec_hbm, skip_ref, st_hbm, dy_hbm, wx_hbm, wb_hbm, wc_hbm,
    out_hbm, gd_ref,
    x_v, b_v, c_v, dec_v, st_v, dy_v, w_v, g_v,
    xt, dyt, bt, ct, xte, dyfs, cum_s, cumt_s, fs_s, te_s, th_s,
    adj1, summ, ra, rt, ob, a_v, tt_s,
    gx, gb, wd, cb, yi, terms, rt2, tsum,
    sl, rl, sr, rr, own, acc, o_v,
    load_sem, w_sem, g_sem, a_send, a_recv, rs_l, rs_r, out_sem,
):
    s = lax.axis_index("seq")
    h = lax.axis_index("head")
    z = h // 2
    core = lax.rem(h, 2)
    sib = (s, h + 1 - 2 * core)
    left = (s, lax.rem(h + HEAD - 2, HEAD))
    right = (s, lax.rem(h + 2, HEAD))

    def peer(o):
        return (lax.rem(s + o, SEQ), h)

    barrier = pltpu.get_barrier_semaphore()

    def greet(o, carry):
        pl.semaphore_signal(barrier, inc=1, device_id=peer(o), device_id_type=MESH)
        return carry

    lax.fori_loop(1, SEQ, greet, 0)
    for other in (sib, left, right):
        pl.semaphore_signal(barrier, inc=1, device_id=other, device_id_type=MESH)

    loads = [
        pltpu.make_async_copy(src, dst, load_sem.at[i])
        for i, (src, dst) in enumerate(
            (
                (dec_hbm, dec_v),
                (dy_hbm, dy_v),
                (c_hbm, c_v),
                (b_hbm, b_v),
                (x_hbm, x_v),
                (st_hbm, st_v),
                (wx_hbm.at[:, core], w_v.at[:, :, 0:HP]),
                (wb_hbm.at[:, core], w_v.at[:, :, HP : HP + N]),
                (wc_hbm.at[:, core], w_v.at[:, :, HP + N : KOWN]),
            )
        )
    ]
    for load in loads:
        load.start()

    row_i = lax.broadcasted_iota(jnp.int32, (Q, Q), 0)
    col_i = lax.broadcasted_iota(jnp.int32, (Q, Q), 1)

    loads[0].wait()
    upto = (row_i <= col_i).astype(f32).astype(bf16)
    log_decay = jnp.log(dec_v[...])
    for k in range(2):
        lanes = slice(k * Q, (k + 1) * Q)
        cum = exact_dot(log_decay[:, lanes], upto)
        cum_s[:, lanes] = cum
        fs_s[:, lanes] = jnp.exp(cum)
        last = jnp.broadcast_to(cum[:, Q - 1 : Q], (NH, Q))
        te_s[:, lanes] = jnp.exp(last - cum)
        th_s[k] = jnp.exp(last[:, 0:N])
    tt_s[...] = th_s[0] * th_s[1]
    rt[0] = tt_s[...]

    loads[1].wait()
    dyt[...] = dy_v[...].T
    for i in range(NH):
        rows = slice(i * PS, (i + 1) * PS)
        dyfs[rows, :] = (dyt[rows, :].astype(f32) * fs_s[i : i + 1, :]).astype(bf16)
    loads[2].wait()
    adj1[...] = dot(dyfs[:, Q : 2 * Q], c_v[Q : 2 * Q, :])
    adj0 = dot(dyfs[:, 0:Q], c_v[0:Q, :])
    for i in range(NH):
        rows = slice(i * PS, (i + 1) * PS)
        summ[rows, :] = (adj0[rows, :] + th_s[0, i : i + 1, :] * adj1[rows, :]).astype(bf16)
    ra[0] = summ[pl.ds(pl.multiple_of(s * SL, SL), SL), :]

    pl.semaphore_wait(barrier, SEQ - 1 + 3)

    def send_slice(o, carry):
        to = lax.rem(s + o, SEQ)
        pltpu.make_async_remote_copy(
            src_ref=summ.at[pl.ds(pl.multiple_of(to * SL, SL), SL)],
            dst_ref=ra.at[SEQ - o],
            send_sem=a_send.at[0],
            recv_sem=a_recv.at[0],
            device_id=(to, h),
            device_id_type=MESH,
        ).start()
        pltpu.make_async_remote_copy(
            src_ref=tt_s,
            dst_ref=rt.at[SEQ - o],
            send_sem=a_send.at[1],
            recv_sem=a_recv.at[1],
            device_id=(to, h),
            device_id_type=MESH,
        ).start()
        return carry

    lax.fori_loop(1, SEQ, send_slice, 0)

    w_copies = [
        pltpu.make_async_remote_copy(
            src_ref=src.at[:, 1 - core],
            dst_ref=w_v.at[:, :, lo:hi],
            send_sem=w_sem.at[0, i],
            recv_sem=w_sem.at[1, i],
            device_id=sib,
            device_id_type=MESH,
        )
        for i, (src, lo, hi) in enumerate(
            (
                (wx_hbm, KOWN, KOWN + HP),
                (wb_hbm, KOWN + HP, KOWN + HP + N),
                (wc_hbm, KOWN + HP + N, 2 * KOWN),
            )
        )
    ]
    for copy in w_copies:
        copy.start()

    loads[4].wait()
    xt[...] = x_v[...].T
    for i in range(NH):
        rows = slice(i * PS, (i + 1) * PS)
        xte[rows, :] = (xt[rows, :].astype(f32) * te_s[i : i + 1, :]).astype(bf16)
    loads[3].wait()
    bt[...] = b_v[...].T
    ct[...] = c_v[...].T
    cumt_s[...] = cum_s[...].T
    loads[5].wait()

    def all_of(ref, i):
        return pltpu.make_async_remote_copy(
            src_ref=ref,
            dst_ref=ref,
            send_sem=a_send.at[i],
            recv_sem=a_recv.at[i],
            device_id=sib,
            device_id_type=MESH,
        )

    for i, ref in ((0, ra), (1, rt)):
        arrived = all_of(ref.at[pl.ds(1, SEQ - 1)], i)
        arrived.wait_recv()
    mine = s // (SEQ // NH)

    def scan(step, cur):
        d = SEQ - 1 - step
        slot = lax.rem(d - s + SEQ, SEQ)
        ob[d] = cur.astype(bf16)
        through = rt[slot, pl.ds(mine, 1), :]
        return ra[slot].astype(f32) + through * cur

    lax.fori_loop(0, SEQ, scan, jnp.zeros((SL, N), f32))
    own_rows = pl.ds(pl.multiple_of(s * SL, SL), SL)
    a_v[own_rows, :] = ob[s]

    def send_back(o, carry):
        to = lax.rem(s + o, SEQ)
        pltpu.make_async_remote_copy(
            src_ref=ob.at[to],
            dst_ref=a_v.at[own_rows],
            send_sem=a_send.at[2],
            recv_sem=a_recv.at[2],
            device_id=(to, h),
            device_id_type=MESH,
        ).start()
        return carry

    lax.fori_loop(1, SEQ, send_back, 0)

    def block(k, carry):
        lanes = pl.ds(pl.multiple_of(k * Q, Q), Q)
        srows = pl.ds(pl.multiple_of(k * HP, HP), HP)
        c_k = c_v[lanes, :]
        bt_k = bt[:, lanes]
        ct_k = ct[:, lanes]
        s0 = st_v[srows, :].astype(bf16)
        cb[...] = dot(c_k, bt_k)
        yi[...] = dot(s0, ct_k)
        causal = row_i >= col_i
        for i in range(NH):
            rows = slice(i * PS, (i + 1) * PS)
            xh = xt[rows, lanes]
            dyh = dyt[rows, lanes]
            gaps = cumt_s[lanes, i : i + 1] - cum_s[i : i + 1, lanes]
            decay = jnp.exp(jnp.where(causal, gaps, -1e30))
            forward = (decay * cb[...]).astype(bf16)
            product = dot(dy_v[lanes, rows], xh)
            if i == 0:
                wd[...] = decay * product
            else:
                wd[...] += decay * product
            gx0 = dot(dyh, forward)
            y = dot(xh, forward, NT) + fs_s[i : i + 1, lanes] * yi[rows, :]
            dyf = dyh.astype(f32)
            terms[i : i + 1, lanes] = jnp.sum(dyf * y - xh.astype(f32) * gx0, axis=0, keepdims=True)
            gx[rows, lanes] = gx0 + skip_ref[i] * dyf
        decayed = wd[...].astype(bf16)
        gb[:, lanes] = dot(ct_k, decayed)
        gc = dot(bt_k, decayed, NT) + dot(s0, dyfs[:, lanes], TN)
        g_v[HP + N : KOWN, lanes] = gc.astype(bf16)
        return carry

    lax.fori_loop(0, 2, block, 0)

    all_of(a_v.at[pl.ds(0, HP - SL)], 2).wait_recv()
    later = a_v[...]
    for k in (1, 0):
        lanes = slice(k * Q, (k + 1) * Q)
        if k == 0:
            later = jnp.concatenate(
                [
                    (
                        adj1[i * PS : (i + 1) * PS, :]
                        + th_s[1, i : i + 1, :] * a_v[i * PS : (i + 1) * PS, :].astype(f32)
                    ).astype(bf16)
                    for i in range(NH)
                ],
                axis=0,
            )
        yi[...] = dot(later, bt[:, lanes])
        g_v[HP : HP + N, lanes] = (gb[:, lanes] + dot(later, xte[:, lanes], TN)).astype(bf16)
        for i in range(NH):
            rows = slice(i * PS, (i + 1) * PS)
            gxr = te_s[i : i + 1, lanes] * yi[rows, :]
            g_v[rows, lanes] = (gx[rows, lanes] + gxr).astype(bf16)
            terms[i : i + 1, lanes] -= jnp.sum(
                xt[rows, lanes].astype(f32) * gxr, axis=0, keepdims=True
            )

    g_copy = pltpu.make_async_remote_copy(
        src_ref=g_v.at[pl.ds(0, KOWN)],
        dst_ref=g_v.at[pl.ds(KOWN, KOWN)],
        send_sem=g_sem.at[0],
        recv_sem=g_sem.at[1],
        device_id=sib,
        device_id_type=MESH,
    )
    g_copy.start()

    for load in loads[6:]:
        load.wait()
    for copy in w_copies:
        copy.wait()
    g_copy.wait()

    def product_of(chunk, row):
        return dot(w_v[chunk, pl.ds(pl.multiple_of(row, TM), TM), :], g_v[...])

    ahead = lax.rem(z + 1, 4)
    behind = lax.rem(z + 3, 4)
    far = lax.rem(z + 2, 4)

    def to_left(stage, j):
        return pltpu.make_async_remote_copy(
            src_ref=sl.at[stage, j],
            dst_ref=rl.at[stage, j],
            send_sem=rs_l.at[0, stage, j],
            recv_sem=rs_l.at[1, stage, j],
            device_id=left,
            device_id_type=MESH,
        )

    def to_right(stage, j):
        return pltpu.make_async_remote_copy(
            src_ref=sr.at[stage, j],
            dst_ref=rr.at[stage, j],
            send_sem=rs_r.at[0, stage, j],
            recv_sem=rs_r.at[1, stage, j],
            device_id=right,
            device_id_type=MESH,
        )

    def far_tiles(j, carry):
        sl[0, j] = product_of(far, j * TM).astype(bf16)
        to_left(0, j).start()
        sr[0, j] = product_of(far, 2 * TM + j * TM).astype(bf16)
        to_right(0, j).start()
        return carry

    lax.fori_loop(0, 2, far_tiles, 0)

    def direct_tiles(j, carry):
        sl[1, j] = product_of(behind, 2 * TM + j * TM).astype(bf16)
        to_left(1, j).start()
        sr[1, j] = product_of(ahead, j * TM).astype(bf16)
        to_right(1, j).start()
        return carry

    lax.fori_loop(0, 2, direct_tiles, 0)

    from_on = (row_i >= col_i).astype(f32).astype(bf16)
    suffix = [exact_dot(terms[:, k * Q : (k + 1) * Q], from_on) for k in range(2)]
    first, second = (jnp.broadcast_to(part[:, 0:1], (NH, N)) for part in suffix)
    tsum[...] = first + second

    def send_sum(o, carry):
        pltpu.make_async_remote_copy(
            src_ref=tsum,
            dst_ref=rt2.at[SEQ - o],
            send_sem=a_send.at[3],
            recv_sem=a_recv.at[3],
            device_id=peer(o),
            device_id_type=MESH,
        ).start()
        return carry

    lax.fori_loop(1, SEQ, send_sum, 0)

    def next_tiles(j, carry):
        acc[0, j] = product_of(behind, j * TM)
        acc[1, j] = product_of(ahead, 2 * TM + j * TM)
        return carry

    lax.fori_loop(0, 2, next_tiles, 0)

    def own_tiles(j, carry):
        own[j] = product_of(z, j * TM)
        return carry

    lax.fori_loop(0, 4, own_tiles, 0)

    for j in range(2):
        to_left(0, j).wait_recv()
        sl[2, j] = (acc[0, j] + rl[0, j].astype(f32)).astype(bf16)
        to_left(2, j).start()
        to_right(0, j).wait_recv()
        sr[2, j] = (acc[1, j] + rr[0, j].astype(f32)).astype(bf16)
        to_right(2, j).start()

    all_of(rt2.at[pl.ds(1, SEQ - 1)], 3).wait_recv()

    def add_later(o, total):
        return total + jnp.where(s + o < SEQ, rt2[o], 0.0)

    running = lax.fori_loop(1, SEQ, add_later, jnp.zeros((NH, N), f32))
    norm = 1.0 / math.sqrt(SEQ * TOK)
    gd_ref[:, Q : 2 * Q] = (suffix[1] + running[:, 0:1]) * norm
    gd_ref[:, 0:Q] = (suffix[0] + (running + second)[:, 0:1]) * norm

    outs = []
    for j in range(2):
        to_right(1, j).wait_recv()
        to_left(2, j).wait_recv()
        a_tile = own[j] + rr[1, j].astype(f32) + rl[2, j].astype(f32)
        o_v[j * TM : (j + 1) * TM, :] = a_tile.astype(bf16)
        to_left(1, j).wait_recv()
        to_right(2, j).wait_recv()
        b_tile = own[2 + j] + rl[1, j].astype(f32) + rr[2, j].astype(f32)
        o_v[(2 + j) * TM : (3 + j) * TM, :] = b_tile.astype(bf16)
        for half in (j, 2 + j):
            rows = pl.ds(half * TM, TM)
            copy = pltpu.make_async_copy(o_v.at[rows], out_hbm.at[rows], out_sem.at[half])
            copy.start()
            outs.append(copy)

    for i, ref in (
        (0, ra.at[pl.ds(1, SEQ - 1)]),
        (1, rt.at[pl.ds(1, SEQ - 1)]),
        (2, ob.at[pl.ds(1, SEQ - 1)]),
        (3, rt2.at[pl.ds(1, SEQ - 1)]),
    ):
        all_of(ref, i).wait_send()
    for stage in range(3):
        for j in range(2):
            to_left(stage, j).wait_send()
            to_right(stage, j).wait_send()
    for copy in outs:
        copy.wait()


def body(x_in, b_proj, c_proj, decay, d_skip, block_states, grad_out, w_x, w_b, w_c):
    any_spec = pl.BlockSpec(memory_space=pl.ANY)
    dma = pltpu.SemaphoreType.DMA
    return pl.pallas_call(
        kernel,
        out_shape=(
            jax.ShapeDtypeStruct((ROWS, TOK), bf16),
            jax.ShapeDtypeStruct((NH, TOK), f32),
        ),
        in_specs=[any_spec] * 4 + [pl.BlockSpec(memory_space=pltpu.SMEM)] + [any_spec] * 5,
        out_specs=(any_spec, pl.BlockSpec(memory_space=pltpu.VMEM)),
        scratch_shapes=[
            pltpu.VMEM((TOK, HP), bf16),
            pltpu.VMEM((TOK, N), bf16),
            pltpu.VMEM((TOK, N), bf16),
            pltpu.VMEM((NH, TOK), f32),
            pltpu.VMEM((2 * HP, N), f32),
            pltpu.VMEM((TOK, HP), bf16),
            pltpu.VMEM((4, ROWS, 2 * KOWN), bf16),
            pltpu.VMEM((2 * KOWN, TOK), bf16),
            pltpu.VMEM((HP, TOK), bf16),
            pltpu.VMEM((HP, TOK), bf16),
            pltpu.VMEM((N, TOK), bf16),
            pltpu.VMEM((N, TOK), bf16),
            pltpu.VMEM((HP, TOK), bf16),
            pltpu.VMEM((HP, TOK), bf16),
            pltpu.VMEM((NH, TOK), f32),
            pltpu.VMEM((TOK, NH), f32),
            pltpu.VMEM((NH, TOK), f32),
            pltpu.VMEM((NH, TOK), f32),
            pltpu.VMEM((2, NH, N), f32),
            pltpu.VMEM((HP, N), f32),
            pltpu.VMEM((HP, N), bf16),
            pltpu.VMEM((SEQ, SL, N), bf16),
            pltpu.VMEM((SEQ, NH, N), f32),
            pltpu.VMEM((SEQ, SL, N), bf16),
            pltpu.VMEM((HP, N), bf16),
            pltpu.VMEM((NH, N), f32),
            pltpu.VMEM((HP, TOK), f32),
            pltpu.VMEM((N, TOK), f32),
            pltpu.VMEM((Q, Q), f32),
            pltpu.VMEM((Q, Q), f32),
            pltpu.VMEM((HP, Q), f32),
            pltpu.VMEM((NH, TOK), f32),
            pltpu.VMEM((SEQ, NH, N), f32),
            pltpu.VMEM((NH, N), f32),
            pltpu.VMEM((3, 2, TM, TOK), bf16),
            pltpu.VMEM((3, 2, TM, TOK), bf16),
            pltpu.VMEM((3, 2, TM, TOK), bf16),
            pltpu.VMEM((3, 2, TM, TOK), bf16),
            pltpu.VMEM((4, TM, TOK), f32),
            pltpu.VMEM((2, 2, TM, TOK), f32),
            pltpu.VMEM((ROWS, TOK), bf16),
            dma((9,)),
            dma((2, 3)),
            dma((2,)),
            dma((4,)),
            dma((4,)),
            dma((2, 3, 2)),
            dma((2, 3, 2)),
            dma((4,)),
        ],
        compiler_params=pltpu.CompilerParams(
            collective_id=0, has_side_effects=True, vmem_limit_bytes=48 * 2**20
        ),
    )(
        x_in,
        b_proj,
        c_proj,
        decay,
        d_skip,
        block_states.reshape(2 * HP, N),
        grad_out,
        w_x.reshape(4, 2, ROWS, HP),
        w_b.reshape(4, 2, ROWS, N),
        w_c.reshape(4, 2, ROWS, N),
    )


def solution(mesh):
    return jax.shard_map(
        body,
        mesh=mesh,
        in_specs=(
            P("seq", "head"),
            P("seq", "head"),
            P("seq", "head"),
            P("head", "seq"),
            P("head"),
            P("seq", "head", None, None),
            P("seq", "head"),
            P(None, "head"),
            P(None, "head"),
            P(None, "head"),
        ),
        out_specs=(P("head", "seq"), P("head", "seq")),
        check_vma=False,
    )
```

time: 379 us -> 77.4 us (0.20)
  the two profiles are of different devices: /device:TPU:64 before, /device:TPU:1 now
where the time goes in v1:
time: 77.4 us; the launch traced here: 77 us
  Pallas kernels  66.2 us (86%)
  local copies, waits for them, and re-layouts  10.1 us (13%)
    pallas_call x1, Pallas kernels, body(): pl.pallas_call(kernel, out_shape=(jax.ShapeDtypeStruct((ROWS, TOK), bf16)...  66.2 us
    unnamed x20, local copies, waits for them, and re-layouts  10.1 us

profile of v1, /device:TPU:1, one launch (start us, length us, event | category | flops | bytes accessed | tf_op | source)
XLA Modules:
  0.0 77.0 jit_solution(6315408434674216873)
XLA Ops:
  0.6 0.0 copy-start
  0.6 1.2 %copy-done = bf16[4096,128]{1,0:T(8,128)(2,1)S(1)} copy-done((bf16[4096,128]{1,0:T(8,128)(2,1)S(1)}, bf16[4096,128]{1,0:T(8,128)(2,1)}, u32[]{:S(2)}) %copy-start) | copy-done | bytes 1048600
  1.9 0.0 copy-start.1
  1.9 1.2 %copy-done.1 = bf16[4096,128]{1,0:T(8,128)(2,1)S(1)} copy-done((bf16[4096,128]{1,0:T(8,128)(2,1)S(1)}, bf16[4096,128]{1,0:T(8,128)(2,1)}, u32[]{:S(2)}) %copy-start.1) | copy-done | bytes 1048600
  3.1 0.0 copy-start.2
  3.1 1.0 %copy-done.2 = bf16[512,512]{1,0:T(8,128)(2,1)S(1)} copy-done((bf16[512,512]{1,0:T(8,128)(2,1)S(1)}, bf16[512,512]{1,0:T(8,128)(2,1)}, u32[]{:S(2)}) %copy-start.2) | copy-done | bytes 524312
  4.1 0.0 copy-start.3
  4.1 1.0 %copy-done.3 = f32[2,8,64,128]{3,2,1,0:T(8,128)S(1)} copy-done((f32[2,8,64,128]{3,2,1,0:T(8,128)S(1)}, f32[2,8,64,128]{3,2,1,0:T(8,128)}, u32[]{:S(2)}) %copy-start.3) | copy-done | bytes 524312
  5.2 0.0 copy-start.4
  5.2 1.0 %copy-done.4 = bf16[512,512]{1,0:T(8,128)(2,1)S(1)} copy-done((bf16[512,512]{1,0:T(8,128)(2,1)S(1)}, bf16[512,512]{1,0:T(8,128)(2,1)}, u32[]{:S(2)}) %copy-start.4) | copy-done | bytes 524312
  6.2 0.0 copy-start.5
  6.2 0.9 %copy-done.5 = bf16[512,128]{1,0:T(8,128)(2,1)S(1)} copy-done((bf16[512,128]{1,0:T(8,128)(2,1)S(1)}, bf16[512,128]{1,0:T(8,128)(2,1)}, u32[]{:S(2)}) %copy-start.5) | copy-done | bytes 131096
  7.1 0.0 copy-start.6
  7.1 0.9 %copy-done.6 = bf16[512,128]{1,0:T(8,128)(2,1)S(1)} copy-done((bf16[512,128]{1,0:T(8,128)(2,1)S(1)}, bf16[512,128]{1,0:T(8,128)(2,1)}, u32[]{:S(2)}) %copy-start.6) | copy-done | bytes 131096
  8.0 0.0 copy-start.7
  8.0 0.7 copy-done.7
  8.7 0.0 copy-start.8
  8.7 0.7 copy-done.8
  9.4 66.2 %shard_map.113 = (bf16[512,512]{1,0:T(8,128)(2,1)S(1)}, f32[8,512]{1,0:T(8,128)S(1)}) custom-call(bf16[512,512]{1,0:T(8,128)(2,1)S(1)} %copy-done.2, bf16[512,128]{1,0:T(8,128)(2,1)S(1)} %copy-done.5, bf16[512,128]{1,0:T(8,128)(2,1)S(1)} %copy-done.6, f32[8,512]{1,0:T(8,128)S(1)} %copy-done.7, f32[8]{0:T(128)S(1)} %copy-done.8, f32[1024,128]{1,0:T(8,128)S(1)} %bitcast.6, ...), custom_call_target="tpu_custom_call" | custom-call | tf_op jit(solution)/shard_map/pallas_call | solution.py:428
  75.6 0.8 %copy.14 = bf16[512,512]{1,0:T(8,128)(2,1)} copy(bf16[512,512]{1,0:T(8,128)(2,1)S(1)} %get-tuple-element.4) | data formatting | bytes 1048576
  76.4 0.6 copy.15
Async XLA Ops:
  0.6 1.2 %copy-start = (bf16[4096,128]{1,0:T(8,128)(2,1)S(1)}, bf16[4096,128]{1,0:T(8,128)(2,1)}, u32[]{:S(2)}) copy-start(bf16[4096,128]{1,0:T(8,128)(2,1)} %param.18) | copy-start | bytes 3145732
  1.9 1.2 %copy-start.1 = (bf16[4096,128]{1,0:T(8,128)(2,1)S(1)}, bf16[4096,128]{1,0:T(8,128)(2,1)}, u32[]{:S(2)}) copy-start(bf16[4096,128]{1,0:T(8,128)(2,1)} %param.19) | copy-start | bytes 3145732
  3.1 1.0 %copy-start.2 = (bf16[512,512]{1,0:T(8,128)(2,1)S(1)}, bf16[512,512]{1,0:T(8,128)(2,1)}, u32[]{:S(2)}) copy-start(bf16[512,512]{1,0:T(8,128)(2,1)} %x_hbm.1) | copy-start | bytes 1572868
  4.1 1.0 %copy-start.3 = (f32[2,8,64,128]{3,2,1,0:T(8,128)S(1)}, f32[2,8,64,128]{3,2,1,0:T(8,128)}, u32[]{:S(2)}) copy-start(f32[2,8,64,128]{3,2,1,0:T(8,128)} %param.15) | copy-start | bytes 1572868
  5.2 1.0 %copy-start.4 = (bf16[512,512]{1,0:T(8,128)(2,1)S(1)}, bf16[512,512]{1,0:T(8,128)(2,1)}, u32[]{:S(2)}) copy-start(bf16[512,512]{1,0:T(8,128)(2,1)} %dy_hbm.1) | copy-start | bytes 1572868
  6.2 0.9 %copy-start.5 = (bf16[512,128]{1,0:T(8,128)(2,1)S(1)}, bf16[512,128]{1,0:T(8,128)(2,1)}, u32[]{:S(2)}) copy-start(bf16[512,128]{1,0:T(8,128)(2,1)} %b_hbm.1) | copy-start | bytes 393220
  7.1 0.9 %copy-start.6 = (bf16[512,128]{1,0:T(8,128)(2,1)S(1)}, bf16[512,128]{1,0:T(8,128)(2,1)}, u32[]{:S(2)}) copy-start(bf16[512,128]{1,0:T(8,128)(2,1)} %c_hbm.1) | copy-start | bytes 393220
  8.0 0.7 copy-start.7
  8.7 0.7 copy-start.8

commit v2 on v1

v2 whole, which is shorter than its diff:
```python
import math

import jax
import jax.numpy as jnp
from jax import lax
from jax.experimental import pallas as pl
from jax.experimental.pallas import tpu as pltpu
from jax.sharding import PartitionSpec as P

SEQ = 32
HEAD = 8
TOK = 512
Q = 256
NH = 8
PS = 64
N = 128
HP = NH * PS
KOWN = HP + 2 * N
ROWS = 512
TM = 128
SL = HP // SEQ

MESH = pl.DeviceIdType.MESH
f32 = jnp.float32
bf16 = jnp.bfloat16

TN = (((0,), (0,)), ((), ()))
NT = (((1,), (1,)), ((), ()))


def dot(a, b, dims=(((1,), (0,)), ((), ()))):
    return lax.dot_general(a, b, dims, preferred_element_type=f32)


def split3(v):
    hi = v.astype(bf16).astype(f32)
    rest = v - hi
    mid = rest.astype(bf16).astype(f32)
    low = rest - mid
    return jnp.concatenate([hi, mid, low], axis=0).astype(bf16)


def exact_dot(v, mask):
    rows = v.shape[0]
    out = dot(split3(v), mask)
    return out[0:rows] + out[rows : 2 * rows] + out[2 * rows : 3 * rows]


def kernel(
    x_hbm, b_hbm, c_hbm, dec_hbm, skip_hbm, st_hbm, dy_hbm, wx_hbm, wb_hbm, wc_hbm,
    out_hbm, gd_hbm,
    x_v, b_v, c_v, dec_v, st_v, dy_v, w_v, g_v,
    xt, dyt, bt, ct, xte, dyfs, cum_s, cumt_s, fs_s, te_s, th0, th1,
    adj1, msg, ra, ob, a_v,
    gx, gb, wd, cb, yi, r_s, terms, rt2, tsum, run_v,
    sl, rl, sr, rr, own, acc, o_v, gd_v, skip_ref,
    load_sem, w_sem, p_sem, a_send, a_recv, rs_l, rs_r, out_sem,
):
    s = lax.axis_index("seq")
    h = lax.axis_index("head")
    z = h // 2
    core = lax.rem(h, 2)
    sib = (s, h + 1 - 2 * core)
    left = (s, lax.rem(h + HEAD - 2, HEAD))
    right = (s, lax.rem(h + 2, HEAD))

    def peer(o):
        return (lax.rem(s + o, SEQ), sib[1])

    barrier = pltpu.get_barrier_semaphore()

    def greet(o, carry):
        pl.semaphore_signal(barrier, inc=1, device_id=peer(o), device_id_type=MESH)
        return carry

    lax.fori_loop(0, SEQ, greet, 0)
    for other in (left, right):
        pl.semaphore_signal(barrier, inc=1, device_id=other, device_id_type=MESH)

    loads = [
        pltpu.make_async_copy(src, dst, load_sem.at[i])
        for i, (src, dst) in enumerate(
            (
                (dec_hbm, dec_v),
                (dy_hbm, dy_v),
                (c_hbm, c_v),
                (b_hbm, b_v),
                (x_hbm, x_v),
                (st_hbm, st_v),
                (wx_hbm.at[:, core], w_v.at[:, :, 0:HP]),
                (wb_hbm.at[:, core], w_v.at[:, :, HP : HP + N]),
                (wc_hbm.at[:, core], w_v.at[:, :, HP + N : KOWN]),
                (skip_hbm, skip_ref),
            )
        )
    ]
    for load in loads:
        load.start()

    row_i = lax.broadcasted_iota(jnp.int32, (Q, Q), 0)
    col_i = lax.broadcasted_iota(jnp.int32, (Q, Q), 1)

    loads[0].wait()
    upto = (row_i <= col_i).astype(f32).astype(bf16)
    log_decay = jnp.log(dec_v[...])
    for k in range(2):
        lanes = slice(k * Q, (k + 1) * Q)
        cum = exact_dot(log_decay[:, lanes], upto)
        cum_s[:, lanes] = cum
        fs_s[:, lanes] = jnp.exp(cum)
        last = jnp.broadcast_to(cum[:, Q - 1 : Q], (NH, Q))
        te_s[0, :, lanes] = jnp.exp(last - cum)
        (th0, th1.at[0])[k][...] = jnp.exp(last[:, 0:N])
    through = th0[...] * th1[0]
    coarse = through.astype(bf16).astype(f32)
    fine = through - coarse
    factors = [
        jnp.concatenate(
            [jnp.broadcast_to(part[i : i + 1, :], (SL // 2, N)) for part in (coarse, fine)], axis=0
        ).astype(bf16)
        for i in range(NH)
    ]

    loads[1].wait()
    dyt[...] = dy_v[...].T
    for i in range(NH):
        rows = slice(i * PS, (i + 1) * PS)
        dyfs[rows, :] = (dyt[rows, :].astype(f32) * fs_s[i : i + 1, :]).astype(bf16)
    loads[2].wait()
    adj1[0] = dot(dyfs[:, Q : 2 * Q], c_v[Q : 2 * Q, :])
    adj0 = dot(dyfs[:, 0:Q], c_v[0:Q, :])
    for i in range(SEQ):
        rows = slice(i * SL, (i + 1) * SL)
        head = i * SL // PS
        msg[i, 0:SL] = (adj0[rows, :] + th0[head : head + 1, :] * adj1[0, rows, :]).astype(bf16)
        msg[i, SL : 2 * SL] = factors[head]

    pl.semaphore_wait(barrier, SEQ + 2)

    def send_slice(o, carry):
        to = lax.rem(s + o, SEQ)
        pltpu.make_async_remote_copy(
            src_ref=msg.at[to],
            dst_ref=ra.at[lax.rem(SEQ - o, SEQ)],
            send_sem=a_send.at[0],
            recv_sem=a_recv.at[0],
            device_id=(to, sib[1]),
            device_id_type=MESH,
        ).start()
        return carry

    lax.fori_loop(0, SEQ, send_slice, 0)

    def to_sib(src, dst, sems, i):
        return pltpu.make_async_remote_copy(
            src_ref=src,
            dst_ref=dst,
            send_sem=sems.at[0, i],
            recv_sem=sems.at[1, i],
            device_id=sib,
            device_id_type=MESH,
        )

    w_copies = [
        to_sib(src.at[:, 1 - core], w_v.at[:, :, lo:hi], w_sem, i)
        for i, (src, lo, hi) in enumerate(
            (
                (wx_hbm, KOWN, KOWN + HP),
                (wb_hbm, KOWN + HP, KOWN + HP + N),
                (wc_hbm, KOWN + HP + N, 2 * KOWN),
            )
        )
    ]
    early = [
        to_sib(ref.at[0], ref.at[1], p_sem, i) for i, ref in enumerate((te_s, th1, adj1, bt, xte))
    ]
    for copy in w_copies:
        copy.start()

    loads[4].wait()
    xt[...] = x_v[...].T
    for i in range(NH):
        rows = slice(i * PS, (i + 1) * PS)
        xte[0, rows, :] = (xt[rows, :].astype(f32) * te_s[0, i : i + 1, :]).astype(bf16)
    loads[3].wait()
    bt[0] = b_v[...].T
    ct[...] = c_v[...].T
    cumt_s[...] = cum_s[...].T

    loads[5].wait()
    loads[9].wait()
    def block(k, carry):
        lanes = pl.ds(pl.multiple_of(k * Q, Q), Q)
        srows = pl.ds(pl.multiple_of(k * HP, HP), HP)
        c_k = c_v[lanes, :]
        bt_k = bt[0, :, lanes]
        ct_k = ct[:, lanes]
        s0 = st_v[srows, :].astype(bf16)
        cb[...] = dot(c_k, bt_k)
        yi[...] = dot(s0, ct_k)
        causal = row_i >= col_i
        for i in range(NH):
            rows = slice(i * PS, (i + 1) * PS)
            xh = xt[rows, lanes]
            dyh = dyt[rows, lanes]
            gaps = cumt_s[lanes, i : i + 1] - cum_s[i : i + 1, lanes]
            decay = jnp.exp(jnp.where(causal, gaps, -1e30))
            forward = (decay * cb[...]).astype(bf16)
            product = dot(dy_v[lanes, rows], xh)
            if i == 0:
                wd[...] = decay * product
            else:
                wd[...] += decay * product
            gx0 = dot(dyh, forward)
            y = dot(xh, forward, NT) + fs_s[i : i + 1, lanes] * yi[rows, :]
            dyf = dyh.astype(f32)
            terms[i : i + 1, lanes] = jnp.sum(dyf * y - xh.astype(f32) * gx0, axis=0, keepdims=True)
            gx[0, rows, lanes] = gx0 + skip_ref[i] * dyf
        decayed = wd[...].astype(bf16)
        gb[0, :, lanes] = dot(ct_k, decayed)
        gc = dot(bt_k, decayed, NT) + dot(s0, dyfs[:, lanes], TN)
        g_v[HP + N : KOWN, lanes] = gc.astype(bf16)
        return carry

    for copy in early:
        copy.start()
    lax.fori_loop(0, 2, block, 0)

    late = [
        to_sib(src, dst, p_sem, 5 + i)
        for i, (src, dst) in enumerate(
            (
                (gx.at[0], gx.at[1]),
                (gb.at[0], gb.at[1]),
                (g_v.at[pl.ds(HP + N, N)], g_v.at[pl.ds(KOWN + HP + N, N)]),
            )
        )
    ]
    for copy in late:
        copy.start()

    def all_of(ref, i):
        return pltpu.make_async_remote_copy(
            src_ref=ref,
            dst_ref=ref,
            send_sem=a_send.at[i],
            recv_sem=a_recv.at[i],
            device_id=sib,
            device_id_type=MESH,
        )

    all_of(ra, 0).wait_recv()

    def scan(step, cur):
        d = SEQ - 1 - step
        slot = lax.rem(d - s + SEQ, SEQ)
        ob[d] = cur.astype(bf16)
        parts = ra[slot, SL : 2 * SL, :].astype(f32)
        factor = parts[0 : SL // 2, :] + parts[SL // 2 : SL, :]
        return ra[slot, 0:SL, :].astype(f32) + jnp.concatenate([factor, factor], axis=0) * cur

    lax.fori_loop(0, SEQ, scan, jnp.zeros((SL, N), f32))
    own_rows = pl.ds(pl.multiple_of(s * SL, SL), SL)

    def send_back(o, carry):
        to = lax.rem(s + o, SEQ)
        pltpu.make_async_remote_copy(
            src_ref=ob.at[to],
            dst_ref=a_v.at[0, own_rows],
            send_sem=a_send.at[1],
            recv_sem=a_recv.at[1],
            device_id=(to, sib[1]),
            device_id_type=MESH,
        ).start()
        return carry

    lax.fori_loop(0, SEQ, send_back, 0)

    all_of(a_v.at[0], 1).wait_recv()
    a_copy = to_sib(a_v.at[0], a_v.at[1], p_sem, 8)
    a_copy.start()

    def with_adjoint(side):
        for k in (1, 0):
            lanes = slice(k * Q, (k + 1) * Q)
            later = a_v[side]
            if k == 0:
                later = jnp.concatenate(
                    [
                        (
                            adj1[side, i * PS : (i + 1) * PS, :]
                            + th1[side, i : i + 1, :]
                            * a_v[side, i * PS : (i + 1) * PS, :].astype(f32)
                        ).astype(bf16)
                        for i in range(NH)
                    ],
                    axis=0,
                )
            r_s[side, :, lanes] = dot(later, bt[side, :, lanes])
            base = side * KOWN
            g_v[base + HP : base + HP + N, lanes] = (
                gb[side, :, lanes] + dot(later, xte[side, :, lanes], TN)
            ).astype(bf16)
            for i in range(NH):
                rows = slice(i * PS, (i + 1) * PS)
                g_v[base + i * PS : base + (i + 1) * PS, lanes] = (
                    gx[side, rows, lanes] + te_s[side, i : i + 1, lanes] * r_s[side, rows, lanes]
                ).astype(bf16)

    with_adjoint(0)
    for load in loads[6:9]:
        load.wait()
    for copy in early + late + w_copies:
        copy.wait()
    a_copy.wait()
    with_adjoint(1)

    def product_of(chunk, row):
        return dot(w_v[chunk, pl.ds(pl.multiple_of(row, TM), TM), :], g_v[...])

    ahead = lax.rem(z + 1, 4)
    behind = lax.rem(z + 3, 4)
    far = lax.rem(z + 2, 4)

    def to_left(stage, j):
        return pltpu.make_async_remote_copy(
            src_ref=sl.at[stage, j],
            dst_ref=rl.at[stage, j],
            send_sem=rs_l.at[0, stage, j],
            recv_sem=rs_l.at[1, stage, j],
            device_id=left,
            device_id_type=MESH,
        )

    def to_right(stage, j):
        return pltpu.make_async_remote_copy(
            src_ref=sr.at[stage, j],
            dst_ref=rr.at[stage, j],
            send_sem=rs_r.at[0, stage, j],
            recv_sem=rs_r.at[1, stage, j],
            device_id=right,
            device_id_type=MESH,
        )

    def far_tiles(j, carry):
        sl[0, j] = product_of(far, j * TM).astype(bf16)
        to_left(0, j).start()
        sr[0, j] = product_of(far, 2 * TM + j * TM).astype(bf16)
        to_right(0, j).start()
        return carry

    lax.fori_loop(0, 2, far_tiles, 0)

    def direct_tiles(j, carry):
        sl[1, j] = product_of(behind, 2 * TM + j * TM).astype(bf16)
        sr[1, j] = product_of(ahead, j * TM).astype(bf16)
        return carry

    lax.fori_loop(0, 2, direct_tiles, 0)

    def follow(stage, j, before, i):
        to_left(before, i).wait_send()
        to_left(stage, j).start()
        to_right(before, i).wait_send()
        to_right(stage, j).start()

    follow(1, 0, 0, 0)

    for i in range(NH):
        rows = slice(i * PS, (i + 1) * PS)
        terms[i : i + 1, :] -= te_s[0, i : i + 1, :] * jnp.sum(
            xt[rows, :].astype(f32) * r_s[0, rows, :], axis=0, keepdims=True
        )
    from_on = (row_i >= col_i).astype(f32).astype(bf16)
    suffix = [exact_dot(terms[:, k * Q : (k + 1) * Q], from_on) for k in range(2)]
    first, second = (jnp.broadcast_to(part[:, 0:1], (NH, N)) for part in suffix)
    head_lane = (
        lax.broadcasted_iota(jnp.int32, (NH, N), 0) == lax.broadcasted_iota(jnp.int32, (NH, N), 1)
    )
    tsum[...] = jnp.sum(jnp.where(head_lane, first + second, 0.0), axis=0, keepdims=True)

    def send_sum(o, carry):
        pltpu.make_async_remote_copy(
            src_ref=tsum,
            dst_ref=rt2.at[SEQ - o],
            send_sem=a_send.at[2],
            recv_sem=a_recv.at[2],
            device_id=peer(o),
            device_id_type=MESH,
        ).start()
        return carry

    lax.fori_loop(1, SEQ, send_sum, 0)

    def next_tiles(j, carry):
        acc[0, j] = product_of(behind, j * TM)
        acc[1, j] = product_of(ahead, 2 * TM + j * TM)
        return carry

    lax.fori_loop(0, 2, next_tiles, 0)

    def own_tiles(j, carry):
        own[j] = product_of(z, j * TM)
        return carry

    lax.fori_loop(0, 4, own_tiles, 0)

    follow(1, 1, 0, 1)

    def add_later(o, total):
        return total + jnp.where(s + o < SEQ, rt2[o], 0.0)

    all_of(rt2.at[pl.ds(1, SEQ - 1)], 2).wait_recv()
    run_v[0] = lax.fori_loop(1, SEQ, add_later, jnp.zeros((1, N), f32))
    run_copy = to_sib(run_v.at[0], run_v.at[1], p_sem, 9)
    run_copy.start()

    for j in range(2):
        to_left(0, j).wait_recv()
        sl[2, j] = (acc[0, j] + rl[0, j].astype(f32)).astype(bf16)
        to_right(0, j).wait_recv()
        sr[2, j] = (acc[1, j] + rr[0, j].astype(f32)).astype(bf16)
        follow(2, j, 1, j)


    run_copy.wait()
    running = jnp.broadcast_to(run_v[1], (NH, N))
    running = jnp.sum(jnp.where(head_lane, running, 0.0), axis=1, keepdims=True)
    norm = 1.0 / math.sqrt(SEQ * TOK)
    gd_v[:, Q : 2 * Q] = (suffix[1] + running) * norm
    gd_v[:, 0:Q] = (suffix[0] + running + second[:, 0:1]) * norm

    outs = [pltpu.make_async_copy(gd_v, gd_hbm, out_sem.at[0])]
    outs[0].start()
    for j in range(2):
        to_right(1, j).wait_recv()
        to_left(2, j).wait_recv()
        a_tile = own[j] + rr[1, j].astype(f32) + rl[2, j].astype(f32)
        o_v[j * TM : (j + 1) * TM, :] = a_tile.astype(bf16)
        to_left(1, j).wait_recv()
        to_right(2, j).wait_recv()
        b_tile = own[2 + j] + rl[1, j].astype(f32) + rr[2, j].astype(f32)
        o_v[(2 + j) * TM : (3 + j) * TM, :] = b_tile.astype(bf16)
        for half in (j, 2 + j):
            rows = pl.ds(half * TM, TM)
            copy = pltpu.make_async_copy(o_v.at[rows], out_hbm.at[rows], out_sem.at[1 + half])
            copy.start()
            outs.append(copy)

    for i, ref in (
        (0, ra),
        (1, ob),
        (2, rt2.at[pl.ds(1, SEQ - 1)]),
    ):
        all_of(ref, i).wait_send()
    for j in range(2):
        to_left(2, j).wait_send()
        to_right(2, j).wait_send()
    for copy in outs:
        copy.wait()


def hand_over(out_in, decays_in, out, decays):
    out[...] = out_in[...]
    decays[...] = decays_in[...]


def body(x_in, b_proj, c_proj, decay, d_skip, block_states, grad_out, w_x, w_b, w_c):
    any_spec = pl.BlockSpec(memory_space=pl.ANY)
    dma = pltpu.SemaphoreType.DMA
    out, decays = pl.pallas_call(
        kernel,
        out_shape=(
            jax.ShapeDtypeStruct((ROWS, TOK), bf16),
            jax.ShapeDtypeStruct((NH, TOK), f32),
        ),
        in_specs=[any_spec] * 10,
        out_specs=(any_spec, any_spec),
        scratch_shapes=[
            pltpu.VMEM((TOK, HP), bf16),
            pltpu.VMEM((TOK, N), bf16),
            pltpu.VMEM((TOK, N), bf16),
            pltpu.VMEM((NH, TOK), f32),
            pltpu.VMEM((2 * HP, N), f32),
            pltpu.VMEM((TOK, HP), bf16),
            pltpu.VMEM((4, ROWS, 2 * KOWN), bf16),
            pltpu.VMEM((2 * KOWN, TOK), bf16),
            pltpu.VMEM((HP, TOK), bf16),
            pltpu.VMEM((HP, TOK), bf16),
            pltpu.VMEM((2, N, TOK), bf16),
            pltpu.VMEM((N, TOK), bf16),
            pltpu.VMEM((2, HP, TOK), bf16),
            pltpu.VMEM((HP, TOK), bf16),
            pltpu.VMEM((NH, TOK), f32),
            pltpu.VMEM((TOK, NH), f32),
            pltpu.VMEM((NH, TOK), f32),
            pltpu.VMEM((2, NH, TOK), f32),
            pltpu.VMEM((NH, N), f32),
            pltpu.VMEM((2, NH, N), f32),
            pltpu.VMEM((2, HP, N), f32),
            pltpu.VMEM((SEQ, 2 * SL, N), bf16),
            pltpu.VMEM((SEQ, 2 * SL, N), bf16),
            pltpu.VMEM((SEQ, SL, N), bf16),
            pltpu.VMEM((2, HP, N), bf16),
            pltpu.VMEM((2, HP, TOK), f32),
            pltpu.VMEM((2, N, TOK), f32),
            pltpu.VMEM((Q, Q), f32),
            pltpu.VMEM((Q, Q), f32),
            pltpu.VMEM((HP, Q), f32),
            pltpu.VMEM((2, HP, TOK), f32),
            pltpu.VMEM((NH, TOK), f32),
            pltpu.VMEM((SEQ, 1, N), f32),
            pltpu.VMEM((1, N), f32),
            pltpu.VMEM((2, 1, N), f32),
            pltpu.VMEM((3, 2, TM, TOK), bf16),
            pltpu.VMEM((3, 2, TM, TOK), bf16),
            pltpu.VMEM((3, 2, TM, TOK), bf16),
            pltpu.VMEM((3, 2, TM, TOK), bf16),
            pltpu.VMEM((4, TM, TOK), f32),
            pltpu.VMEM((2, 2, TM, TOK), f32),
            pltpu.VMEM((ROWS, TOK), bf16),
            pltpu.VMEM((NH, TOK), f32),
            pltpu.SMEM((NH,), f32),
            dma((10,)),
            dma((2, 3)),
            dma((2, 10)),
            dma((3,)),
            dma((3,)),
            dma((2, 3, 2)),
            dma((2, 3, 2)),
            dma((5,)),
        ],
        compiler_params=pltpu.CompilerParams(
            collective_id=0, has_side_effects=True, vmem_limit_bytes=60 * 2**20
        ),
    )(
        x_in,
        b_proj,
        c_proj,
        decay,
        d_skip,
        block_states.reshape(2 * HP, N),
        grad_out,
        w_x.reshape(4, 2, ROWS, HP),
        w_b.reshape(4, 2, ROWS, N),
        w_c.reshape(4, 2, ROWS, N),
    )
    return pl.pallas_call(
        hand_over,
        out_shape=(
            jax.ShapeDtypeStruct((ROWS, TOK), bf16),
            jax.ShapeDtypeStruct((NH, TOK), f32),
        ),
    )(out, decays)


def solution(mesh):
    return jax.shard_map(
        body,
        mesh=mesh,
        in_specs=(
            P("seq", "head"),
            P("seq", "head"),
            P("seq", "head"),
            P("head", "seq"),
            P("head"),
            P("seq", "head", None, None),
            P("seq", "head"),
            P(None, "head"),
            P(None, "head"),
            P(None, "head"),
        ),
        out_specs=(P("head", "seq"), P("head", "seq")),
        check_vma=False,
    )
```

time: 77.4 us -> 66.2 us (0.86)
  the two profiles are of different devices: /device:TPU:1 before, /device:TPU:33 now
where the time goes in v2:
time: 66.2 us; the launch traced here: 66 us
  Pallas kernels  65.4 us (99%)
    pallas_call x1, Pallas kernels, body(): pl.pallas_call(kernel, out_shape=(jax.ShapeDtypeStruct((ROWS, TOK), bf16)...  63.5 us
    pallas_call x1, Pallas kernels, body(): pl.pallas_call(hand_over, out_shape=(jax.ShapeDtypeStruct((ROWS, TOK), bf...  1.87 us

profile of v2, /device:TPU:33, one launch (start us, length us, event | category | flops | bytes accessed | tf_op | source)
XLA Modules:
  0.0 66.0 jit_solution(18181711466844304745)
XLA Ops:
  0.6 63.5 %shard_map.113 = (bf16[512,512]{1,0:T(8,128)(2,1)}, f32[8,512]{1,0:T(8,128)}) custom-call(bf16[512,512]{1,0:T(8,128)(2,1)} %x_hbm.1, bf16[512,128]{1,0:T(8,128)(2,1)} %b_hbm.1, bf16[512,128]{1,0:T(8,128)(2,1)} %c_hbm.1, f32[8,512]{1,0:T(8,128)} %dec_hbm.1, f32[8]{0:T(128)} %skip_hbm.1, f32[1024,128]{1,0:T(8,128)} %bitcast.7, bf16[512,512]{1,0:T(8,128)(2,1)} %dy_hbm.1, ...), custom_call_target="tpu_custom_call" | custom-call | tf_op jit(solution)/shard_map/pallas_call | solution.py:471
  64.2 1.9 %shard_map.114 = (bf16[512,512]{1,0:T(8,128)(2,1)}, f32[8,512]{1,0:T(8,128)}) custom-call(bf16[512,512]{1,0:T(8,128)(2,1)} %get-tuple-element.4.out_in, f32[8,512]{1,0:T(8,128)} %get-tuple-element.5.decays_in), custom_call_target="tpu_custom_call" | custom-call | tf_op jit(solution)/shard_map/pallas_call | solution.py:548

commit v3 on v2

--- a/solution.py
+++ b/solution.py
@@ -19,6 +19,12 @@
 ROWS = 512
 TM = 128
 SL = HP // SEQ
+
+NZ, NX, NY = 2, 4, 4
+STEPS = sorted(
+    ((a, b, c) for a in range(NZ) for b in range(NX) for c in range(NY)),
+    key=lambda t: -(min(t[0], NZ - t[0]) + min(t[1], NX - t[1]) + min(t[2], NY - t[2])),
+)
 
 MESH = pl.DeviceIdType.MESH
 f32 = jnp.float32
@@ -64,16 +70,34 @@
     left = (s, lax.rem(h + HEAD - 2, HEAD))
     right = (s, lax.rem(h + 2, HEAD))
 
-    def peer(o):
-        return (lax.rem(s + o, SEQ), sib[1])
+    at_z, at_x, at_y = s // (NX * NY), lax.rem(s // NY, NX), lax.rem(s, NY)
+
+    def peer_at(step):
+        return (
+            lax.rem(at_z + step[0], NZ) * (NX * NY)
+            + lax.rem(at_x + step[1], NX) * NY
+            + lax.rem(at_y + step[2], NY)
+        )
+
+    def slot_at(step):
+        a, b, c = ((size - i) % size for size, i in zip((NZ, NX, NY), step))
+        return (a * NX + b) * NY + c
+
+    def slot_of(d):
+        return (
+            lax.rem(d // (NX * NY) - at_z + NZ, NZ) * (NX * NY)
+            + lax.rem(lax.rem(d // NY, NX) - at_x + NX, NX) * NY
+            + lax.rem(lax.rem(d, NY) - at_y + NY, NY)
+        )
 
     barrier = pltpu.get_barrier_semaphore()
 
-    def greet(o, carry):
-        pl.semaphore_signal(barrier, inc=1, device_id=peer(o), device_id_type=MESH)
-        return carry
-
-    lax.fori_loop(0, SEQ, greet, 0)
+    for step in STEPS:
+        other = (peer_at(step), sib[1])
+        pl.semaphore_signal(barrier, inc=1, device_id=other, device_id_type=MESH)
+        if any(step):
+            other = (peer_at(step), h)
+            pl.semaphore_signal(barrier, inc=1, device_id=other, device_id_type=MESH)
     for other in (left, right):
         pl.semaphore_signal(barrier, inc=1, device_id=other, device_id_type=MESH)
 
@@ -135,21 +159,18 @@
         msg[i, 0:SL] = (adj0[rows, :] + th0[head : head + 1, :] * adj1[0, rows, :]).astype(bf16)
         msg[i, SL : 2 * SL] = factors[head]
 
-    pl.semaphore_wait(barrier, SEQ + 2)
-
-    def send_slice(o, carry):
-        to = lax.rem(s + o, SEQ)
+    pl.semaphore_wait(barrier, 2 * SEQ + 1)
+
+    for step in STEPS:
+        to = peer_at(step)
         pltpu.make_async_remote_copy(
             src_ref=msg.at[to],
-            dst_ref=ra.at[lax.rem(SEQ - o, SEQ)],
+            dst_ref=ra.at[slot_at(step)],
             send_sem=a_send.at[0],
             recv_sem=a_recv.at[0],
             device_id=(to, sib[1]),
             device_id_type=MESH,
         ).start()
-        return carry
-
-    lax.fori_loop(0, SEQ, send_slice, 0)
 
     def to_sib(src, dst, sems, i):
         return pltpu.make_async_remote_copy(
@@ -253,17 +274,20 @@
 
     def scan(step, cur):
         d = SEQ - 1 - step
-        slot = lax.rem(d - s + SEQ, SEQ)
+        slot = slot_of(d)
         ob[d] = cur.astype(bf16)
         parts = ra[slot, SL : 2 * SL, :].astype(f32)
         factor = parts[0 : SL // 2, :] + parts[SL // 2 : SL, :]
         return ra[slot, 0:SL, :].astype(f32) + jnp.concatenate([factor, factor], axis=0) * cur
 
-    lax.fori_loop(0, SEQ, scan, jnp.zeros((SL, N), f32))
+    cur = jnp.zeros((SL, N), f32)
+    for step in range(SEQ):
+        cur = scan(step, cur)
     own_rows = pl.ds(pl.multiple_of(s * SL, SL), SL)
 
-    def send_back(o, carry):
-        to = lax.rem(s + o, SEQ)
+    a_v[1, own_rows, :] = ob[s]
+    for step in STEPS:
+        to = peer_at(step)
         pltpu.make_async_remote_copy(
             src_ref=ob.at[to],
             dst_ref=a_v.at[0, own_rows],
@@ -272,13 +296,17 @@
             device_id=(to, sib[1]),
             device_id_type=MESH,
         ).start()
-        return carry
-
-    lax.fori_loop(0, SEQ, send_back, 0)
+        if any(step):
+            pltpu.make_async_remote_copy(
+                src_ref=ob.at[to],
+                dst_ref=a_v.at[1, own_rows],
+                send_sem=a_send.at[3],
+                recv_sem=a_recv.at[3],
+                device_id=(to, h),
+                device_id_type=MESH,
+            ).start()
 
     all_of(a_v.at[0], 1).wait_recv()
-    a_copy = to_sib(a_v.at[0], a_v.at[1], p_sem, 8)
-    a_copy.start()
 
     def with_adjoint(side):
         for k in (1, 0):
@@ -312,7 +340,7 @@
         load.wait()
     for copy in early + late + w_copies:
         copy.wait()
-    a_copy.wait()
+    all_of(a_v.at[1, pl.ds(0, HP - SL)], 3).wait_recv()
     with_adjoint(1)
 
     def product_of(chunk, row):
@@ -385,7 +413,7 @@
             dst_ref=rt2.at[SEQ - o],
             send_sem=a_send.at[2],
             recv_sem=a_recv.at[2],
-            device_id=peer(o),
+            device_id=(lax.rem(s + o, SEQ), sib[1]),
             device_id_type=MESH,
         ).start()
         return carry
@@ -412,7 +440,7 @@
 
     all_of(rt2.at[pl.ds(1, SEQ - 1)], 2).wait_recv()
     run_v[0] = lax.fori_loop(1, SEQ, add_later, jnp.zeros((1, N), f32))
-    run_copy = to_sib(run_v.at[0], run_v.at[1], p_sem, 9)
+    run_copy = to_sib(run_v.at[0], run_v.at[1], p_sem, 8)
     run_copy.start()
 
     for j in range(2):
@@ -450,6 +478,7 @@
     for i, ref in (
         (0, ra),
         (1, ob),
+        (3, ob.at[pl.ds(1, SEQ - 1)]),
         (2, rt2.at[pl.ds(1, SEQ - 1)]),
     ):
         all_of(ref, i).wait_send()
@@ -523,9 +552,9 @@
             pltpu.SMEM((NH,), f32),
             dma((10,)),
             dma((2, 3)),
-            dma((2, 10)),
-            dma((3,)),
-            dma((3,)),
+            dma((2, 9)),
+            dma((4,)),
+            dma((4,)),
             dma((2, 3, 2)),
             dma((2, 3, 2)),
             dma((5,)),

time: 66.2 us -> 64.2 us (0.970)
  Pallas kernels: 65.4 us -> 63.4 us
    pallas_call x1, Pallas kernels: 63.5 us -> 61.6 us  [body(): pl.pallas_call(kernel, out_shape=(jax.ShapeDtypeStruct((ROWS, TOK), bf16)...]
where the time goes in v3:
time: 64.2 us; the launch traced here: 64.1 us
  Pallas kernels  63.4 us (99%)
    pallas_call x1, Pallas kernels, body(): pl.pallas_call(kernel, out_shape=(jax.ShapeDtypeStruct((ROWS, TOK), bf16)...  61.6 us
    pallas_call x1, Pallas kernels, body(): pl.pallas_call(hand_over, out_shape=(jax.ShapeDtypeStruct((ROWS, TOK), bf...  1.87 us

profile of v3, /device:TPU:33, one launch (start us, length us, event | category | flops | bytes accessed | tf_op | source)
XLA Modules:
  0.0 64.1 jit_solution(3438072466155942094)
XLA Ops:
  0.6 61.6 %shard_map.113 = (bf16[512,512]{1,0:T(8,128)(2,1)}, f32[8,512]{1,0:T(8,128)}) custom-call(bf16[512,512]{1,0:T(8,128)(2,1)} %x_hbm.1, bf16[512,128]{1,0:T(8,128)(2,1)} %b_hbm.1, bf16[512,128]{1,0:T(8,128)(2,1)} %c_hbm.1, f32[8,512]{1,0:T(8,128)} %dec_hbm.1, f32[8]{0:T(128)} %skip_hbm.1, f32[1024,128]{1,0:T(8,128)} %bitcast.7, bf16[512,512]{1,0:T(8,128)(2,1)} %dy_hbm.1, ...), custom_call_target="tpu_custom_call" | custom-call | tf_op jit(solution)/shard_map/pallas_call | solution.py:500
  62.2 1.9 %shard_map.114 = (bf16[512,512]{1,0:T(8,128)(2,1)}, f32[8,512]{1,0:T(8,128)}) custom-call(bf16[512,512]{1,0:T(8,128)(2,1)} %get-tuple-element.4.out_in, f32[8,512]{1,0:T(8,128)} %get-tuple-element.5.decays_in), custom_call_target="tpu_custom_call" | custom-call | tf_op jit(solution)/shard_map/pallas_call | solution.py:577

commit v4 on v3

--- a/solution.py
+++ b/solution.py
@@ -54,10 +54,10 @@
 
 def kernel(
     x_hbm, b_hbm, c_hbm, dec_hbm, skip_hbm, st_hbm, dy_hbm, wx_hbm, wb_hbm, wc_hbm,
-    out_hbm, gd_hbm,
+    out_hbm, last_hbm, gd_hbm,
     x_v, b_v, c_v, dec_v, st_v, dy_v, w_v, g_v,
     xt, dyt, bt, ct, xte, dyfs, cum_s, cumt_s, fs_s, te_s, th0, th1,
-    adj1, msg, ra, ob, a_v,
+    adj1, msg, ra, tt_s, rt, ob, a_v,
     gx, gb, wd, cb, yi, r_s, terms, rt2, tsum, run_v,
     sl, rl, sr, rr, own, acc, o_v, gd_v, skip_ref,
     load_sem, w_sem, p_sem, a_send, a_recv, rs_l, rs_r, out_sem,
@@ -136,14 +136,8 @@
         te_s[0, :, lanes] = jnp.exp(last - cum)
         (th0, th1.at[0])[k][...] = jnp.exp(last[:, 0:N])
     through = th0[...] * th1[0]
-    coarse = through.astype(bf16).astype(f32)
-    fine = through - coarse
-    factors = [
-        jnp.concatenate(
-            [jnp.broadcast_to(part[i : i + 1, :], (SL // 2, N)) for part in (coarse, fine)], axis=0
-        ).astype(bf16)
-        for i in range(NH)
-    ]
+    for i in range(NH):
+        tt_s[i] = through[i : i + 1, :]
 
     loads[1].wait()
     dyt[...] = dy_v[...].T
@@ -156,8 +150,7 @@
     for i in range(SEQ):
         rows = slice(i * SL, (i + 1) * SL)
         head = i * SL // PS
-        msg[i, 0:SL] = (adj0[rows, :] + th0[head : head + 1, :] * adj1[0, rows, :]).astype(bf16)
-        msg[i, SL : 2 * SL] = factors[head]
+        msg[i] = (adj0[rows, :] + th0[head : head + 1, :] * adj1[0, rows, :]).astype(bf16)
 
     pl.semaphore_wait(barrier, 2 * SEQ + 1)
 
@@ -168,6 +161,14 @@
             dst_ref=ra.at[slot_at(step)],
             send_sem=a_send.at[0],
             recv_sem=a_recv.at[0],
+            device_id=(to, sib[1]),
+            device_id_type=MESH,
+        ).start()
+        pltpu.make_async_remote_copy(
+            src_ref=tt_s.at[to // (SEQ // NH)],
+            dst_ref=rt.at[slot_at(step)],
+            send_sem=a_send.at[4],
+            recv_sem=a_recv.at[4],
             device_id=(to, sib[1]),
             device_id_type=MESH,
         ).start()
@@ -271,14 +272,13 @@
         )
 
     all_of(ra, 0).wait_recv()
+    all_of(rt, 4).wait_recv()
 
     def scan(step, cur):
         d = SEQ - 1 - step
         slot = slot_of(d)
         ob[d] = cur.astype(bf16)
-        parts = ra[slot, SL : 2 * SL, :].astype(f32)
-        factor = parts[0 : SL // 2, :] + parts[SL // 2 : SL, :]
-        return ra[slot, 0:SL, :].astype(f32) + jnp.concatenate([factor, factor], axis=0) * cur
+        return ra[slot].astype(f32) + rt[slot] * cur
 
     cur = jnp.zeros((SL, N), f32)
     for step in range(SEQ):
@@ -351,9 +351,10 @@
     far = lax.rem(z + 2, 4)
 
     def to_left(stage, j):
+        landing = last_hbm.at[pl.ds(j * TM, TM)] if stage == 2 else rl.at[stage, j]
         return pltpu.make_async_remote_copy(
             src_ref=sl.at[stage, j],
-            dst_ref=rl.at[stage, j],
+            dst_ref=landing,
             send_sem=rs_l.at[0, stage, j],
             recv_sem=rs_l.at[1, stage, j],
             device_id=left,
@@ -361,9 +362,10 @@
         )
 
     def to_right(stage, j):
+        landing = last_hbm.at[pl.ds((2 + j) * TM, TM)] if stage == 2 else rr.at[stage, j]
         return pltpu.make_async_remote_copy(
             src_ref=sr.at[stage, j],
-            dst_ref=rr.at[stage, j],
+            dst_ref=landing,
             send_sem=rs_r.at[0, stage, j],
             recv_sem=rs_r.at[1, stage, j],
             device_id=right,
@@ -462,13 +464,9 @@
     outs[0].start()
     for j in range(2):
         to_right(1, j).wait_recv()
-        to_left(2, j).wait_recv()
-        a_tile = own[j] + rr[1, j].astype(f32) + rl[2, j].astype(f32)
-        o_v[j * TM : (j + 1) * TM, :] = a_tile.astype(bf16)
+        o_v[j * TM : (j + 1) * TM, :] = (own[j] + rr[1, j].astype(f32)).astype(bf16)
         to_left(1, j).wait_recv()
-        to_right(2, j).wait_recv()
-        b_tile = own[2 + j] + rl[1, j].astype(f32) + rr[2, j].astype(f32)
-        o_v[(2 + j) * TM : (3 + j) * TM, :] = b_tile.astype(bf16)
+        o_v[(2 + j) * TM : (3 + j) * TM, :] = (own[2 + j] + rl[1, j].astype(f32)).astype(bf16)
         for half in (j, 2 + j):
             rows = pl.ds(half * TM, TM)
             copy = pltpu.make_async_copy(o_v.at[rows], out_hbm.at[rows], out_sem.at[1 + half])
@@ -477,6 +475,7 @@
 
     for i, ref in (
         (0, ra),
+        (4, rt),
         (1, ob),
         (3, ob.at[pl.ds(1, SEQ - 1)]),
         (2, rt2.at[pl.ds(1, SEQ - 1)]),
@@ -487,24 +486,28 @@
         to_right(2, j).wait_send()
     for copy in outs:
         copy.wait()
-
-
-def hand_over(out_in, decays_in, out, decays):
-    out[...] = out_in[...]
+    for j in range(2):
+        to_left(2, j).wait_recv()
+        to_right(2, j).wait_recv()
+
+
+def hand_over(most, last, decays_in, out, decays):
+    out[...] = (most[...].astype(f32) + last[...].astype(f32)).astype(bf16)
     decays[...] = decays_in[...]
 
 
 def body(x_in, b_proj, c_proj, decay, d_skip, block_states, grad_out, w_x, w_b, w_c):
     any_spec = pl.BlockSpec(memory_space=pl.ANY)
     dma = pltpu.SemaphoreType.DMA
-    out, decays = pl.pallas_call(
+    most, last, decays = pl.pallas_call(
         kernel,
         out_shape=(
+            jax.ShapeDtypeStruct((ROWS, TOK), bf16),
             jax.ShapeDtypeStruct((ROWS, TOK), bf16),
             jax.ShapeDtypeStruct((NH, TOK), f32),
         ),
         in_specs=[any_spec] * 10,
-        out_specs=(any_spec, any_spec),
+        out_specs=(any_spec, any_spec, any_spec),
         scratch_shapes=[
             pltpu.VMEM((TOK, HP), bf16),
             pltpu.VMEM((TOK, N), bf16),
@@ -527,8 +530,10 @@
             pltpu.VMEM((NH, N), f32),
             pltpu.VMEM((2, NH, N), f32),
             pltpu.VMEM((2, HP, N), f32),
-            pltpu.VMEM((SEQ, 2 * SL, N), bf16),
-            pltpu.VMEM((SEQ, 2 * SL, N), bf16),
+            pltpu.VMEM((SEQ, SL, N), bf16),
+            pltpu.VMEM((SEQ, SL, N), bf16),
+            pltpu.VMEM((NH, 1, N), f32),
+            pltpu.VMEM((SEQ, 1, N), f32),
             pltpu.VMEM((SEQ, SL, N), bf16),
             pltpu.VMEM((2, HP, N), bf16),
             pltpu.VMEM((2, HP, TOK), f32),
@@ -542,9 +547,9 @@
             pltpu.VMEM((1, N), f32),
             pltpu.VMEM((2, 1, N), f32),
             pltpu.VMEM((3, 2, TM, TOK), bf16),
+            pltpu.VMEM((2, 2, TM, TOK), bf16),
             pltpu.VMEM((3, 2, TM, TOK), bf16),
-            pltpu.VMEM((3, 2, TM, TOK), bf16),
-            pltpu.VMEM((3, 2, TM, TOK), bf16),
+            pltpu.VMEM((2, 2, TM, TOK), bf16),
             pltpu.VMEM((4, TM, TOK), f32),
             pltpu.VMEM((2, 2, TM, TOK), f32),
             pltpu.VMEM((ROWS, TOK), bf16),
@@ -553,8 +558,8 @@
             dma((10,)),
             dma((2, 3)),
             dma((2, 9)),
-            dma((4,)),
-            dma((4,)),
+            dma((5,)),
+            dma((5,)),
             dma((2, 3, 2)),
             dma((2, 3, 2)),
             dma((5,)),
@@ -580,7 +585,7 @@
             jax.ShapeDtypeStruct((ROWS, TOK), bf16),
             jax.ShapeDtypeStruct((NH, TOK), f32),
         ),
-    )(out, decays)
+    )(most, last, decays)
 
 
 def solution(mesh):

time: 64.2 us -> 63.4 us (0.988)
  Pallas kernels: 63.4 us -> 62.6 us
    pallas_call x1, Pallas kernels: 61.6 us -> 60.4 us  [body(): pl.pallas_call(kernel, out_shape=(jax.ShapeDtypeStruct((ROWS, TOK), bf16)...]
where the time goes in v4:
time: 63.4 us; the launch traced here: 63.2 us
  Pallas kernels  62.6 us (99%)
  between operations  0.64 us (1%)
    pallas_call x1, Pallas kernels, body(): pl.pallas_call(kernel, out_shape=(jax.ShapeDtypeStruct((ROWS, TOK), bf16)...  60.4 us
    pallas_call x1, Pallas kernels, body(): pl.pallas_call(hand_over, out_shape=(jax.ShapeDtypeStruct((ROWS, TOK), bf...  2.12 us

profile of v4, /device:TPU:33, one launch (start us, length us, event | category | flops | bytes accessed | tf_op | source)
XLA Modules:
  0.0 63.2 jit_solution(12002485526634529006)
XLA Ops:
  0.6 60.4 %shard_map.113 = (bf16[512,512]{1,0:T(8,128)(2,1)}, bf16[512,512]{1,0:T(8,128)(2,1)}, f32[8,512]{1,0:T(8,128)}) custom-call(bf16[512,512]{1,0:T(8,128)(2,1)} %x_hbm.1, bf16[512,128]{1,0:T(8,128)(2,1)} %b_hbm.1, bf16[512,128]{1,0:T(8,128)(2,1)} %c_hbm.1, f32[8,512]{1,0:T(8,128)} %dec_hbm.1, f32[8]{0:T(128)} %skip_hbm.1, f32[1024,128]{1,0:T(8,128)} %bitcast.7, ...), custom_call_target="tpu_custom_call" | custom-call | tf_op jit(solution)/shard_map/pallas_call | solution.py:502
  61.1 2.1 %shard_map.114 = (bf16[512,512]{1,0:T(8,128)(2,1)}, f32[8,512]{1,0:T(8,128)}) custom-call(bf16[512,512]{1,0:T(8,128)(2,1)} %get-tuple-element.5.most, bf16[512,512]{1,0:T(8,128)(2,1)} %get-tuple-element.6.last, f32[8,512]{1,0:T(8,128)} %get-tuple-element.7.decays_in), custom_call_target="tpu_custom_call" | custom-call | tf_op jit(solution)/shard_map/pallas_call | solution.py:582

commit v5 on v4

--- a/solution.py
+++ b/solution.py
@@ -90,17 +90,6 @@
             + lax.rem(lax.rem(d, NY) - at_y + NY, NY)
         )
 
-    barrier = pltpu.get_barrier_semaphore()
-
-    for step in STEPS:
-        other = (peer_at(step), sib[1])
-        pl.semaphore_signal(barrier, inc=1, device_id=other, device_id_type=MESH)
-        if any(step):
-            other = (peer_at(step), h)
-            pl.semaphore_signal(barrier, inc=1, device_id=other, device_id_type=MESH)
-    for other in (left, right):
-        pl.semaphore_signal(barrier, inc=1, device_id=other, device_id_type=MESH)
-
     loads = [
         pltpu.make_async_copy(src, dst, load_sem.at[i])
         for i, (src, dst) in enumerate(
@@ -118,7 +107,21 @@
             )
         )
     ]
-    for load in loads:
+    for load in loads[:3]:
+        load.start()
+
+    barrier = pltpu.get_barrier_semaphore()
+
+    for step in STEPS:
+        other = (peer_at(step), sib[1])
+        pl.semaphore_signal(barrier, inc=1, device_id=other, device_id_type=MESH)
+        if any(step):
+            other = (peer_at(step), h)
+            pl.semaphore_signal(barrier, inc=1, device_id=other, device_id_type=MESH)
+    for other in (left, right):
+        pl.semaphore_signal(barrier, inc=1, device_id=other, device_id_type=MESH)
+
+    for load in loads[3:]:
         load.start()
 
     row_i = lax.broadcasted_iota(jnp.int32, (Q, Q), 0)
@@ -324,7 +327,9 @@
                     ],
                     axis=0,
                 )
-            r_s[side, :, lanes] = dot(later, bt[side, :, lanes])
+            back = dot(later, bt[side, :, lanes])
+            if side == 0:
+                r_s[:, lanes] = back
             base = side * KOWN
             g_v[base + HP : base + HP + N, lanes] = (
                 gb[side, :, lanes] + dot(later, xte[side, :, lanes], TN)
@@ -332,7 +337,7 @@
             for i in range(NH):
                 rows = slice(i * PS, (i + 1) * PS)
                 g_v[base + i * PS : base + (i + 1) * PS, lanes] = (
-                    gx[side, rows, lanes] + te_s[side, i : i + 1, lanes] * r_s[side, rows, lanes]
+                    gx[side, rows, lanes] + te_s[side, i : i + 1, lanes] * back[rows, :]
                 ).astype(bf16)
 
     with_adjoint(0)
@@ -399,7 +404,7 @@
     for i in range(NH):
         rows = slice(i * PS, (i + 1) * PS)
         terms[i : i + 1, :] -= te_s[0, i : i + 1, :] * jnp.sum(
-            xt[rows, :].astype(f32) * r_s[0, rows, :], axis=0, keepdims=True
+            xt[rows, :].astype(f32) * r_s[rows, :], axis=0, keepdims=True
         )
     from_on = (row_i >= col_i).astype(f32).astype(bf16)
     suffix = [exact_dot(terms[:, k * Q : (k + 1) * Q], from_on) for k in range(2)]
@@ -493,7 +498,10 @@
 
 def hand_over(most, last, decays_in, out, decays):
     out[...] = (most[...].astype(f32) + last[...].astype(f32)).astype(bf16)
-    decays[...] = decays_in[...]
+
+    @pl.when(pl.program_id(0) == 0)
+    def _():
+        decays[...] = decays_in[...]
 
 
 def body(x_in, b_proj, c_proj, decay, d_skip, block_states, grad_out, w_x, w_b, w_c):
@@ -541,7 +549,7 @@
             pltpu.VMEM((Q, Q), f32),
             pltpu.VMEM((Q, Q), f32),
             pltpu.VMEM((HP, Q), f32),
-            pltpu.VMEM((2, HP, TOK), f32),
+            pltpu.VMEM((HP, TOK), f32),
             pltpu.VMEM((NH, TOK), f32),
             pltpu.VMEM((SEQ, 1, N), f32),
             pltpu.VMEM((1, N), f32),
@@ -579,12 +587,17 @@
         w_b.reshape(4, 2, ROWS, N),
         w_c.reshape(4, 2, ROWS, N),
     )
+    block = pl.BlockSpec((ROWS // 2, TOK), lambda i: (i, 0))
+    whole = pl.BlockSpec((NH, TOK), lambda i: (0, 0))
     return pl.pallas_call(
         hand_over,
         out_shape=(
             jax.ShapeDtypeStruct((ROWS, TOK), bf16),
             jax.ShapeDtypeStruct((NH, TOK), f32),
         ),
+        grid=(2,),
+        in_specs=(block, block, whole),
+        out_specs=(block, whole),
     )(most, last, decays)
 
 

time: 63.4 us -> 63.2 us (level)
  no operation moved by 1% of the time
where the time goes in v5:
time: 63.2 us; the launch traced here: 63 us
  Pallas kernels  62.4 us (99%)
  between operations  0.64 us (1%)
    pallas_call x1, Pallas kernels, body(): pl.pallas_call(kernel, out_shape=(jax.ShapeDtypeStruct((ROWS, TOK), bf16)...  60.4 us
    pallas_call x1, Pallas kernels, body(): pl.pallas_call(hand_over, out_shape=(jax.ShapeDtypeStruct((ROWS, TOK), bf...  1.99 us

profile of v5, /device:TPU:33, one launch (start us, length us, event | category | flops | bytes accessed | tf_op | source)
XLA Modules:
  0.0 63.0 jit_solution(9295543301270553065)
XLA Ops:
  0.6 60.4 %shard_map.113 = (bf16[512,512]{1,0:T(8,128)(2,1)}, bf16[512,512]{1,0:T(8,128)(2,1)}, f32[8,512]{1,0:T(8,128)}) custom-call(bf16[512,512]{1,0:T(8,128)(2,1)} %x_hbm.1, bf16[512,128]{1,0:T(8,128)(2,1)} %b_hbm.1, bf16[512,128]{1,0:T(8,128)(2,1)} %c_hbm.1, f32[8,512]{1,0:T(8,128)} %dec_hbm.1, f32[8]{0:T(128)} %skip_hbm.1, f32[1024,128]{1,0:T(8,128)} %bitcast.7, ...), custom_call_target="tpu_custom_call" | custom-call | tf_op jit(solution)/shard_map/pallas_call | solution.py:510
  61.0 2.0 %shard_map.114 = (bf16[512,512]{1,0:T(8,128)(2,1)}, f32[8,512]{1,0:T(8,128)}) custom-call(bf16[512,512]{1,0:T(8,128)(2,1)} %get-tuple-element.5.most, bf16[512,512]{1,0:T(8,128)(2,1)} %get-tuple-element.6.last, f32[8,512]{1,0:T(8,128)} %get-tuple-element.7.decays_in), custom_call_target="tpu_custom_call" | custom-call | tf_op jit(solution)/shard_map/pallas_call | solution.py:592
